TPU v7x, 256 devices: a whole 4x4x8 slice. The times are simulated.
256 devices in a mesh: dp: 16 (over x_hi, z), ctx: 16 (over y, x_lo, core).
Axes of the slice: x: 4 (x_hi: 2, x_lo: 2; x = x_hi * 2 + x_lo), y: 4, z: 8, core: 2. Of those that a mesh axis runs over, the one named last changes fastest.
Arguments:
- query: bfloat16 [16, 512, 4096], P('dp', None, 'ctx'), may hold values from -6 to 6
- key_act: bfloat16 [16, 512, 4096], P('dp', None, 'ctx'), may hold values from -6 to 6
- value_act: bfloat16 [16, 512, 4096], P('dp', None, 'ctx'), may hold values from -6 to 6
- filter_taps: float32 [512, 4096], P(None, 'ctx'), may hold values from -2 to 2
- grad_out: bfloat16 [16, 512, 4096], P('dp', None, 'ctx'), may hold values from -6 to 6
Outputs:
- output: bfloat16 [16, 512, 4096], P('dp', None, 'ctx')
- grad_query: bfloat16 [16, 512, 4096], P('dp', None, 'ctx')
- grad_key: bfloat16 [16, 512, 4096], P('dp', None, 'ctx')
- grad_value: bfloat16 [16, 512, 4096], P('dp', None, 'ctx')
- grad_filter: float32 [512, 4096], P(None, 'ctx')
All inputs are finite; a program needn't handle non-finite values.
Results may differ from a plain program's by a relative error of at most 0.0011.
Values sent between devices are 32-bit elements; how exact they have to be, the bound alone decides.
A program may use at most 128 MiB of HBM per device.

v0:
```python
import math

import jax
import jax.numpy as jnp
from jax import lax
from jax.sharding import PartitionSpec as P

PRECISE = lax.Precision.HIGHEST


def angle_table(first, second, modulus):
    product = first[:, None] * second[None, :] % modulus
    return product.astype(jnp.float32) * (2.0 * math.pi / modulus)


def square_table(length):
    indices = jnp.arange(length, dtype=jnp.int32)
    angles = angle_table(indices, indices, length)
    return (jnp.cos(angles), jnp.sin(angles))


def largest_factor(length):
    chosen = 1
    for factor in range(1, math.isqrt(length) + 1):
        if length % factor == 0:
            chosen = factor
    return chosen


def forward_spectrum(signal):
    ctx_size = lax.axis_size("ctx")
    rows_count, length = signal.shape
    piece = length // ctx_size
    double = 2 * ctx_size
    modulus = double * length
    first_dim = largest_factor(length)
    second_dim = length // first_dim
    freq_steps = jnp.arange(double, dtype=jnp.int32)
    block_steps = jnp.arange(ctx_size, dtype=jnp.int32)
    block_angles = angle_table(freq_steps, block_steps, double)
    block_cos = jnp.cos(block_angles)
    block_sin = jnp.sin(block_angles)
    columns = signal.reshape(rows_count, ctx_size, piece)
    across_columns = lax.all_to_all(columns, "ctx", split_axis=1, concat_axis=1, tiled=True)
    real_part = jnp.einsum("kd,rds->rks", block_cos, across_columns, precision=PRECISE)
    imag_part = -jnp.einsum("kd,rds->rks", block_sin, across_columns, precision=PRECISE)
    positions = lax.axis_index("ctx") * piece + jnp.arange(piece, dtype=jnp.int32)
    twist = angle_table(freq_steps, positions, modulus)
    twist_cos = jnp.cos(twist)
    twist_sin = jnp.sin(twist)
    real_part, imag_part = (
        real_part * twist_cos + imag_part * twist_sin,
        imag_part * twist_cos - real_part * twist_sin,
    )
    real_part, imag_part = (
        lax.all_to_all(real_part, "ctx", split_axis=1, concat_axis=2, tiled=True),
        lax.all_to_all(imag_part, "ctx", split_axis=1, concat_axis=2, tiled=True),
    )
    real_part = real_part.reshape(rows_count, 2, first_dim, second_dim)
    imag_part = imag_part.reshape(rows_count, 2, first_dim, second_dim)
    first_cos, first_sin = square_table(first_dim)
    second_cos, second_sin = square_table(second_dim)
    upper_real = jnp.einsum("ka,rjab->rjkb", first_cos, real_part, precision=PRECISE) + jnp.einsum(
        "ka,rjab->rjkb", first_sin, imag_part, precision=PRECISE
    )
    upper_imag = jnp.einsum("ka,rjab->rjkb", first_cos, imag_part, precision=PRECISE) - jnp.einsum(
        "ka,rjab->rjkb", first_sin, real_part, precision=PRECISE
    )
    inner = angle_table(
        jnp.arange(first_dim, dtype=jnp.int32), jnp.arange(second_dim, dtype=jnp.int32), length
    )
    inner_cos = jnp.cos(inner)
    inner_sin = jnp.sin(inner)
    turned_real = upper_real * inner_cos + upper_imag * inner_sin
    turned_imag = upper_imag * inner_cos - upper_real * inner_sin
    final_real = jnp.einsum(
        "rjab,bk->rjak", turned_real, second_cos, precision=PRECISE
    ) + jnp.einsum("rjab,bk->rjak", turned_imag, second_sin, precision=PRECISE)
    final_imag = jnp.einsum(
        "rjab,bk->rjak", turned_imag, second_cos, precision=PRECISE
    ) - jnp.einsum("rjab,bk->rjak", turned_real, second_sin, precision=PRECISE)
    return (final_real, final_imag)


def inverse_spectrum(real_part, imag_part):
    ctx_size = lax.axis_size("ctx")
    rows_count, pair_count, first_dim, second_dim = real_part.shape
    length = first_dim * second_dim
    piece = length // ctx_size
    double = 2 * ctx_size
    modulus = double * length
    first_cos, first_sin = square_table(first_dim)
    second_cos, second_sin = square_table(second_dim)
    upper_real = jnp.einsum("rjak,bk->rjab", real_part, second_cos, precision=PRECISE) - jnp.einsum(
        "rjak,bk->rjab", imag_part, second_sin, precision=PRECISE
    )
    upper_imag = jnp.einsum("rjak,bk->rjab", imag_part, second_cos, precision=PRECISE) + jnp.einsum(
        "rjak,bk->rjab", real_part, second_sin, precision=PRECISE
    )
    inner = angle_table(
        jnp.arange(first_dim, dtype=jnp.int32), jnp.arange(second_dim, dtype=jnp.int32), length
    )
    inner_cos = jnp.cos(inner)
    inner_sin = jnp.sin(inner)
    turned_real = upper_real * inner_cos - upper_imag * inner_sin
    turned_imag = upper_imag * inner_cos + upper_real * inner_sin
    time_real = jnp.einsum("ka,rjkb->rjab", first_cos, turned_real, precision=PRECISE) - jnp.einsum(
        "ka,rjkb->rjab", first_sin, turned_imag, precision=PRECISE
    )
    time_imag = jnp.einsum("ka,rjkb->rjab", first_cos, turned_imag, precision=PRECISE) + jnp.einsum(
        "ka,rjkb->rjab", first_sin, turned_real, precision=PRECISE
    )
    time_real = time_real.reshape(rows_count, pair_count, length)
    time_imag = time_imag.reshape(rows_count, pair_count, length)
    freq_steps = jnp.arange(double, dtype=jnp.int32)
    block_steps = jnp.arange(ctx_size, dtype=jnp.int32)
    block_angles = angle_table(freq_steps, block_steps, double)
    block_cos = jnp.cos(block_angles)
    block_sin = jnp.sin(block_angles)
    column_real = lax.all_to_all(time_real, "ctx", split_axis=2, concat_axis=1, tiled=True)
    column_imag = lax.all_to_all(time_imag, "ctx", split_axis=2, concat_axis=1, tiled=True)
    positions = lax.axis_index("ctx") * piece + jnp.arange(piece, dtype=jnp.int32)
    twist = angle_table(freq_steps, positions, modulus)
    twist_cos = jnp.cos(twist)
    twist_sin = jnp.sin(twist)
    plain_real = column_real * twist_cos - column_imag * twist_sin
    plain_imag = column_imag * twist_cos + column_real * twist_sin
    values = jnp.einsum("kd,rks->rds", block_cos, plain_real, precision=PRECISE) - jnp.einsum(
        "kd,rks->rds", block_sin, plain_imag, precision=PRECISE
    )
    spatial = values * (1.0 / modulus)
    timeline = lax.all_to_all(spatial, "ctx", split_axis=1, concat_axis=2, tiled=True)
    return timeline.reshape(rows_count, length)


def complex_product(left_real, left_imag, right_real, right_imag, conjugate_left):
    if conjugate_left:
        return (
            left_real * right_real + left_imag * right_imag,
            left_real * right_imag - left_imag * right_real,
        )
    return (
        left_real * right_real - left_imag * right_imag,
        left_real * right_imag + left_imag * right_real,
    )


def shards(query, key_act, value_act, filter_taps, grad_out):
    batch_local, channels, length = query.shape
    rows_count = batch_local * channels
    dp_size = lax.axis_size("dp")
    ctx_size = lax.axis_size("ctx")
    share = channels // dp_size
    query32 = query.astype(jnp.float32).reshape(rows_count, length)
    key32 = key_act.astype(jnp.float32).reshape(rows_count, length)
    value32 = value_act.astype(jnp.float32).reshape(rows_count, length)
    grad32 = grad_out.astype(jnp.float32).reshape(rows_count, length)
    mixed = key32 * value32
    own_taps = lax.dynamic_slice_in_dim(filter_taps, lax.axis_index("dp") * share, share, 0)
    stacked_real, stacked_imag = forward_spectrum(jnp.concatenate([mixed, own_taps], axis=0))
    filt_real, filt_imag = (
        lax.all_gather(stacked_real[rows_count:], "dp", axis=0, tiled=True),
        lax.all_gather(stacked_imag[rows_count:], "dp", axis=0, tiled=True),
    )
    spec_shape = stacked_real.shape[1:]
    batched_shape = (batch_local, channels) + spec_shape
    z_real = stacked_real[:rows_count].reshape(batched_shape)
    z_imag = stacked_imag[:rows_count].reshape(batched_shape)
    conv_real, conv_imag = complex_product(z_real, z_imag, filt_real[None], filt_imag[None], False)
    conv = inverse_spectrum(
        conv_real.reshape((rows_count,) + spec_shape), conv_imag.reshape((rows_count,) + spec_shape)
    )
    output = (query32 * conv).astype(jnp.bfloat16)
    dconv = query32 * grad32
    dconv_real, dconv_imag = forward_spectrum(dconv)
    dconv_real = dconv_real.reshape(batched_shape)
    dconv_imag = dconv_imag.reshape(batched_shape)
    dmix_real, dmix_imag = complex_product(
        filt_real[None], filt_imag[None], dconv_real, dconv_imag, True
    )
    dmix_real = dmix_real.reshape((rows_count,) + spec_shape)
    dmix_imag = dmix_imag.reshape((rows_count,) + spec_shape)
    term_real, term_imag = complex_product(z_real, z_imag, dconv_real, dconv_imag, True)
    term_real = jnp.sum(term_real, axis=0)
    term_imag = jnp.sum(term_imag, axis=0)
    scale = 1.0 / math.sqrt(length * ctx_size * batch_local * dp_size)
    shared_real, shared_imag = (
        lax.psum_scatter(term_real, "dp", scatter_dimension=0, tiled=True),
        lax.psum_scatter(term_imag, "dp", scatter_dimension=0, tiled=True),
    )
    inverted = inverse_spectrum(
        jnp.concatenate([dmix_real, shared_real], axis=0),
        jnp.concatenate([dmix_imag, shared_imag], axis=0),
    )
    dmixed = inverted[:rows_count]
    grad_filter = lax.all_gather(inverted[rows_count:] * scale, "dp", axis=0, tiled=True)
    out_shape = (batch_local, channels, length)
    grad_query = (grad32 * conv).astype(jnp.bfloat16)
    grad_key = (dmixed * value32).astype(jnp.bfloat16)
    grad_value = (dmixed * key32).astype(jnp.bfloat16)
    return (
        output.reshape(out_shape),
        grad_query.reshape(out_shape),
        grad_key.reshape(out_shape),
        grad_value.reshape(out_shape),
        grad_filter,
    )


def solution(mesh):
    in_specs = (
        P("dp", None, "ctx"),
        P("dp", None, "ctx"),
        P("dp", None, "ctx"),
        P(None, "ctx"),
        P("dp", None, "ctx"),
    )
    out_specs = (
        P("dp", None, "ctx"),
        P("dp", None, "ctx"),
        P("dp", None, "ctx"),
        P("dp", None, "ctx"),
        P(None, "ctx"),
    )
    return jax.shard_map(shards, mesh=mesh, in_specs=in_specs, out_specs=out_specs, check_vma=False)
```

profile of v0, /device:TPU:6, one launch (start us, length us, event | category | flops | bytes accessed | tf_op | source)
XLA Modules:
  0.0 955.6 jit_solution(11536170795761420383)
XLA Ops:
  11.5 5.9 all-to-all-start
  18.8 9.8 %all-to-all-done = f32[544,16,16]{0,2,1:T(8,128)S(1)} async-done(((f32[544,16,16]{0,2,1:T(8,128)}), f32[544,16,16]{0,2,1:T(8,128)S(1)}, u32[]{:S(2)}, u32[]{:S(2)}) %all-to-all-start) | async-done | bytes 557088 | tf_op jit(solution)/shard_map/all_to_all | solution.py:44
  28.6 4.6 all-to-all-start.6
  34.6 2.7 multiply_subtract_fusion.2
  39.1 3.9 all-to-all-done.6
  43.1 4.8 all-to-all-start.1
  49.7 16.4 %all-to-all-done.1 = f32[544,32,16]{0,2,1:T(8,128)S(1)} async-done(((f32[544,32,16]{0,2,1:T(8,128)}), f32[544,32,16]{0,2,1:T(8,128)S(1)}, u32[]{:S(2)}, u32[]{:S(2)}) %all-to-all-start.1) | async-done | bytes 1114144 | tf_op jit(solution)/shard_map/all_to_all | solution.py:56
  66.1 4.9 all-to-all-start.2
  71.3 2.3 convolution_bitcast_fusion.1
  73.6 3.1 fusion.12
  76.6 12.6 %all-to-all-done.2 = f32[544,32,16]{0,2,1:T(8,128)S(1)} async-done(((f32[544,32,16]{0,2,1:T(8,128)}), f32[544,32,16]{0,2,1:T(8,128)S(1)}, u32[]{:S(2)}, u32[]{:S(2)}) %all-to-all-start.2) | async-done | bytes 1114144 | tf_op jit(solution)/shard_map/all_to_all | solution.py:57
  93.3 2.4 multiply_add_fusion.1
  101.7 2.6 multiply_add_fusion.5
  105.9 4.8 all-to-all-start.8
  110.9 2.8 copy.235
  113.7 15.5 %all-to-all-done.8 = f32[512,32,16]{0,2,1:T(8,128)S(1)} async-done(((f32[512,32,16]{0,2,1:T(8,128)}), f32[512,32,16]{0,2,1:T(8,128)S(1)}, u32[]{:S(2)}, u32[]{:S(2)}) %all-to-all-start.8) | async-done | bytes 1048608 | tf_op jit(solution)/shard_map/all_to_all | solution.py:57
  130.1 8.0 all-to-all-start.7
  138.1 3.9 fusion.49
  149.5 4.1 all-to-all-done.7
  153.6 2.8 fusion.53
  156.4 2.9 fusion.55
  159.3 3.5 fusion.48
  168.2 75.4 %all-gather.3.cloned.1.call-done = f32[512,2,16,16]{3,2,1,0:T(8,128)} async-done(((f32[32,2,16,16]{3,2,1,0:T(8,128)}), f32[512,2,16,16]{3,2,1,0:T(8,128)}) %all-gather.3.cloned.1.call-update) | async-done | bytes 1048592 | tf_op jit(solution)/shard_map/all_gather | solution.py:162
  243.6 6.4 copy.206
  250.0 129.4 %all-gather.5.cloned.1.call-done = f32[512,2,16,16]{3,2,1,0:T(8,128)} async-done(((f32[32,2,16,16]{3,2,1,0:T(8,128)}), f32[512,2,16,16]{3,2,1,0:T(8,128)}) %all-gather.5.cloned.1.call-update) | async-done | bytes 1048592 | tf_op jit(solution)/shard_map/all_gather | solution.py:163
  379.4 6.0 copy.210
  385.5 7.4 multiply_add_fusion.3
  392.8 3.0 copy.313
  395.9 2.6 copy.311
  410.4 6.1 all-to-all-start.3
  422.4 169.7 %reduce-scatter.9.cloned.1.call-done = f32[32,512]{1,0:T(8,128)} async-done(((f32[512,512]{1,0:T(8,128)}), f32[32,512]{1,0:T(8,128)}) %reduce-scatter.9.cloned.1.call-update) | async-done | bytes 65552
  593.0 199.7 %reduce-scatter.7.cloned.1.call-done = f32[32,512]{1,0:T(8,128)} async-done(((f32[512,512]{1,0:T(8,128)}), f32[32,512]{1,0:T(8,128)}) %reduce-scatter.7.cloned.1.call-update) | async-done | bytes 65552
  793.7 2.4 fusion.45
  796.1 2.4 fusion.46
  798.5 2.4 fusion.43
  800.8 2.4 fusion.44
  803.2 6.1 all-to-all-start.4
  809.3 4.7 multiply_add_fusion
  819.1 5.4 all-to-all-done.4
  824.6 5.6 all-to-all-start.10
  835.2 13.3 %all-to-all-done.10 = f32[544,2,256]{0,1,2:T(2,128)} async-done(((f32[544,2,256]{0,1,2:T(2,128)}), f32[544,2,256]{0,1,2:T(2,128)}, u32[]{:S(2)}, u32[]{:S(2)}) %all-to-all-start.10) | async-done | bytes 1114144 | tf_op jit(solution)/shard_map/all_to_all | solution.py:121
  848.5 5.9 all-to-all-start.9
  868.8 3.8 all-to-all-done.9
  872.6 5.8 all-to-all-start.5
  881.9 2.2 all_to_all.142
  888.1 4.9 all-to-all-start.11
  895.9 8.3 all-to-all-done.11
  906.2 41.6 %all_gather.11 = f32[512,256]{1,0:T(8,128)S(1)} all-gather(f32[32,256]{1,0:T(8,128)S(1)} %copy.268), channel_id=1, replica_groups=mesh['dp'=16,'ctx'=16] {'dp'}, dimensions={0}, use_global_device_ids=true | all-gather | bytes 557056 | tf_op jit(solution)/shard_map/all_gather | solution.py:196
  (143 shorter events, 93.7 us)
Async XLA Ops:
  7.2 1.1 copy-start
  10.5 1.0 copy-start.18
  10.6 6.9 copy-start.24
  10.6 7.0 copy-start.25
  11.5 17.1 %all-to-all-start = ((f32[544,16,16]{0,2,1:T(8,128)}), f32[544,16,16]{0,2,1:T(8,128)S(1)}, u32[]{:S(2)}, u32[]{:S(2)}) async-start(f32[544,16,16]{0,2,1:T(8,128)} %bitcast.1), calls=%async_computation | async-start | bytes 1310720 | tf_op jit(solution)/shard_map/all_to_all | solution.py:44
  17.7 11.0 %copy-start.20 = (bf16[1,512,256]{1,2,0:T(8,128)(2,1)}, bf16[1,512,256]{1,2,0:T(8,128)(2,1)S(1)}, u32[]{:S(2)}) copy-start(bf16[1,512,256]{1,2,0:T(8,128)(2,1)S(1)} %copy.189) | copy-start | bytes 786436
  17.8 10.8 %copy-start.22 = (bf16[1,512,256]{1,2,0:T(8,128)(2,1)}, bf16[1,512,256]{1,2,0:T(8,128)(2,1)S(1)}, u32[]{:S(2)}) copy-start(bf16[1,512,256]{1,2,0:T(8,128)(2,1)S(1)} %copy.232) | copy-start | bytes 786436
  28.6 14.4 %all-to-all-start.6 = ((f32[512,16,16]{0,2,1:T(8,128)}), f32[512,16,16]{0,2,1:T(8,128)S(1)}, u32[]{:S(2)}, u32[]{:S(2)}) async-start(f32[512,16,16]{0,2,1:T(8,128)} %bitcast.36), calls=%async_computation.6 | async-start | bytes 1048576 | tf_op jit(solution)/shard_map/all_to_all | solution.py:44
  39.1 8.7 copy-start.11
  43.1 23.0 %all-to-all-start.1 = ((f32[544,32,16]{0,2,1:T(8,128)}), f32[544,32,16]{0,2,1:T(8,128)S(1)}, u32[]{:S(2)}, u32[]{:S(2)}) async-start(f32[544,32,16]{0,2,1:T(8,128)} %copy.195), calls=%async_computation.1 | async-start | bytes 2621440 | tf_op jit(solution)/shard_map/all_to_all | solution.py:56
  66.1 23.1 %all-to-all-start.2 = ((f32[544,32,16]{0,2,1:T(8,128)}), f32[544,32,16]{0,2,1:T(8,128)S(1)}, u32[]{:S(2)}, u32[]{:S(2)}) async-start(f32[544,32,16]{0,2,1:T(8,128)} %copy.198), calls=%async_computation.2 | async-start | bytes 2621440 | tf_op jit(solution)/shard_map/all_to_all | solution.py:57
  71.0 172.7 %all-gather.3.cloned.1.call-start = ((), (), s32[]{:S(2)}) async-start(), calls=%async_computation.14 | async-start | bytes 8912896 | tf_op jit(solution)/shard_map/all_gather | solution.py:162
  89.2 2.0 copy-start.12
  95.7 1.6 copy-start.2
  99.3 1.1 copy-start.13
  100.4 1.3 copy-start.15
  105.9 23.3 %all-to-all-start.8 = ((f32[512,32,16]{0,2,1:T(8,128)}), f32[512,32,16]{0,2,1:T(8,128)S(1)}, u32[]{:S(2)}, u32[]{:S(2)}) async-start(f32[512,32,16]{0,2,1:T(8,128)} %copy.238), calls=%async_computation.8 | async-start | bytes 2097152 | tf_op jit(solution)/shard_map/all_to_all | solution.py:57
  129.2 1.0 copy-start.4
  130.1 23.5 %all-to-all-start.7 = ((f32[512,32,16]{0,2,1:T(8,128)}), f32[512,32,16]{0,2,1:T(8,128)}, u32[]{:S(2)}, u32[]{:S(2)}) async-start(f32[512,32,16]{0,2,1:T(8,128)} %copy.235), calls=%async_computation.7 | async-start | bytes 2097152 | tf_op jit(solution)/shard_map/all_to_all | solution.py:56
  138.1 3.9 copy-start.3
  138.1 241.4 %all-gather.5.cloned.1.call-start = ((), (), s32[]{:S(2)}) async-start(), calls=%async_computation.15 | async-start | bytes 8912896 | tf_op jit(solution)/shard_map/all_gather | solution.py:163
  145.2 1.1 copy-start.14
  146.3 1.5 copy-start.5
  147.6 444.5 %reduce-scatter.9.cloned.1.call-start = ((), (), s32[]{:S(2)}) async-start(), calls=%async_computation.17 | async-start | bytes 1114112
  156.4 2.9 copy-start.17
  162.8 3.3 copy-start.10
  392.8 5.6 copy-start.6
  395.8 396.9 %reduce-scatter.7.cloned.1.call-start = ((), (), s32[]{:S(2)}) async-start(), calls=%async_computation.16 | async-start | bytes 1114112
  400.6 1.2 copy-start.16
  401.8 1.2 copy-start.7
  410.4 392.8 %all-to-all-start.3 = ((f32[512,2,256]{0,1,2:T(2,128)}), f32[512,2,256]{0,1,2:T(2,128)}, u32[]{:S(2)}, u32[]{:S(2)}) async-start(f32[512,2,256]{0,1,2:T(2,128)} %copy.222), calls=%async_computation.3 | async-start | bytes 2097152 | tf_op jit(solution)/shard_map/all_to_all | solution.py:120
  420.6 373.1 %copy-start.9 = (f32[512,2,16,16]{0,3,2,1:T(8,128)S(1)}, f32[512,2,16,16]{0,3,2,1:T(8,128)}, u32[]{:S(2)}) copy-start(f32[512,2,16,16]{0,3,2,1:T(8,128)} %get-tuple-element.37) | copy-start | bytes 3145732
  796.1 2.4 copy-start.8
  803.2 21.4 %all-to-all-start.4 = ((f32[512,2,256]{0,1,2:T(2,128)}), f32[512,2,256]{0,1,2:T(2,128)}, u32[]{:S(2)}, u32[]{:S(2)}) async-start(f32[512,2,256]{0,1,2:T(2,128)} %copy.228), calls=%async_computation.4 | async-start | bytes 2097152 | tf_op jit(solution)/shard_map/all_to_all | solution.py:121
  824.6 23.9 %all-to-all-start.10 = ((f32[544,2,256]{0,1,2:T(2,128)}), f32[544,2,256]{0,1,2:T(2,128)}, u32[]{:S(2)}, u32[]{:S(2)}) async-start(f32[544,2,256]{0,1,2:T(2,128)} %copy.264), calls=%async_computation.10 | async-start | bytes 2621440 | tf_op jit(solution)/shard_map/all_to_all | solution.py:121
  848.5 24.1 %all-to-all-start.9 = ((f32[544,2,256]{0,1,2:T(2,128)}), f32[544,2,256]{0,1,2:T(2,128)}, u32[]{:S(2)}, u32[]{:S(2)}) async-start(f32[544,2,256]{0,1,2:T(2,128)} %copy.260), calls=%async_computation.9 | async-start | bytes 2621440 | tf_op jit(solution)/shard_map/all_to_all | solution.py:120
  872.6 15.5 %all-to-all-start.5 = ((f32[512,16,16]{0,2,1:T(8,128)}), f32[512,16,16]{0,2,1:T(8,128)}, u32[]{:S(2)}, u32[]{:S(2)}) async-start(f32[512,16,16]{0,2,1:T(8,128)} %copy.231), calls=%async_computation.5 | async-start | bytes 1048576 | tf_op jit(solution)/shard_map/all_to_all | solution.py:132
  886.2 6.9 copy-start.21
  886.2 6.9 copy-start.23
  888.1 16.1 %all-to-all-start.11 = ((f32[544,16,16]{0,2,1:T(8,128)}), f32[544,16,16]{0,2,1:T(8,128)S(1)}, u32[]{:S(2)}, u32[]{:S(2)}) async-start(f32[544,16,16]{0,2,1:T(8,128)} %copy.267), calls=%async_computation.11 | async-start | bytes 1310720 | tf_op jit(solution)/shard_map/all_to_all | solution.py:132
  894.2 10.0 %copy-start.19 = (bf16[1,512,256]{1,2,0:T(8,128)(2,1)S(1)}, bf16[1,512,256]{1,2,0:T(8,128)(2,1)}, u32[]{:S(2)}) copy-start(bf16[1,512,256]{1,2,0:T(8,128)(2,1)} %copy-done.18) | copy-start | bytes 786436
  904.4 44.1 %copy-start.1 = (f32[512,256]{1,0:T(8,128)S(1)}, f32[512,256]{1,0:T(8,128)}, u32[]{:S(2)}) copy-start(f32[512,256]{1,0:T(8,128)} %param.8) | copy-start | bytes 1572868
Sparse Core Ops, SparseCore 0:
  101.8 141.7 all-gather.2
  246.8 132.6 all-gather.4
  395.9 196.0 reduce-scatter.8
  595.8 196.9 reduce-scatter.6
where the time goes:
time: 963 us; the launch traced here: 956 us
  waiting for transfers between devices  668 us (69%)
  matrix products  80.4 us (8%)
  local copies, waits for them, and re-layouts  70.9 us (7%)
  starting transfers between devices  68 us (7%)
  blocking collectives  41.6 us (4%)
  between operations  15 us (2%)
  other arithmetic  11.5 us (1%)
    unnamed x6, waiting for transfers between devices  369 us
    all_gather x1, waiting for transfers between devices, shards(): lax.all_gather(stacked_imag[rows_count:], 'dp', axis=0, tiled=True)  129 us
    all_gather x1, waiting for transfers between devices, shards(): lax.all_gather(stacked_real[rows_count:], 'dp', axis=0, tiled=True)  75.4 us
    all_gather x1, blocking collectives, shards(): lax.all_gather(inverted[rows_count:] * scale, 'dp', axis=0, tiled=True)  41.6 us
    all_to_all x2, waiting for transfers between devices, forward_spectrum(): lax.all_to_all(imag_part, 'ctx', split_axis=1, concat_axis=2, tiled=True)  28.1 us
    all_to_all x2, waiting for transfers between devices, forward_spectrum(): lax.all_to_all(real_part, 'ctx', split_axis=1, concat_axis=2, tiled=True)  20.5 us
  transfers between devices with their start and end apart: 16, of which 15 were waited for; matrix products, arithmetic and copies ran while one was open for 12% of the time, Pallas kernels for 0%

commit v1 on v0

v1 whole, which is shorter than its diff:
```python
import functools
import math

import jax
import jax.numpy as jnp
import numpy as np
from jax import lax
from jax.experimental import pallas as pl
from jax.experimental.pallas import tpu as pltpu
from jax.sharding import PartitionSpec as P

MESH = pl.DeviceIdType.MESH
LANES = 128
RADIX = 64
HALF = RADIX // 2
KEPT = HALF + 1


def turn(value, numerator, denominator):
    real, imag = value
    numerator %= denominator
    eighth = numerator * 8
    if eighth % denominator == 0:
        step = eighth // denominator
        if step == 0:
            return (real, imag)
        if step == 2:
            return (imag, -real)
        if step == 4:
            return (-real, -imag)
        if step == 6:
            return (-imag, real)
        root = math.sqrt(0.5)
        if step == 1:
            return ((real + imag) * root, (imag - real) * root)
        if step == 3:
            return ((imag - real) * root, (real + imag) * -root)
        if step == 5:
            return ((real + imag) * -root, (real - imag) * root)
        return ((real - imag) * root, (real + imag) * root)
    cos = math.cos(2.0 * math.pi * numerator / denominator)
    sin = math.sin(2.0 * math.pi * numerator / denominator)
    return (real * cos + imag * sin, imag * cos - real * sin)


def complex_fft(values, sign):
    size = len(values)
    if size == 1:
        return values
    even = complex_fft(values[0::2], sign)
    odd = complex_fft(values[1::2], sign)
    low, high = [], []
    for k in range(size // 2):
        real, imag = turn(odd[k], sign * k, size)
        low.append((even[k][0] + real, even[k][1] + imag))
        high.append((even[k][0] - real, even[k][1] - imag))
    return low + high


def odd_forward(values):
    quarter = len(values) // 2
    order = 4 * quarter
    packed = [turn((values[n], -values[n + quarter]), n, order) for n in range(quarter)]
    out = complex_fft(packed, 1)
    found = {}
    for j in range(quarter):
        k = 4 * j + 1
        if k < order // 2:
            found[k] = out[j]
        else:
            found[order - k] = (out[j][0], -out[j][1])
    return found


def real_forward(values):
    size = len(values)
    if size == 2:
        return {0: (values[0] + values[1], None), 1: (values[0] - values[1], None)}
    half = size // 2
    evens = real_forward([values[n] + values[n + half] for n in range(half)])
    found = {2 * k: value for k, value in evens.items()}
    found.update(odd_forward([values[n] - values[n + half] for n in range(half)]))
    return found


def padded_forward(values):
    found = {2 * k: value for k, value in real_forward(values).items()}
    found.update(odd_forward(values))
    return found


def odd_inverse(found, order):
    quarter = order // 4
    packed = []
    for j in range(quarter):
        k = 4 * j + 1
        if k < order // 2:
            packed.append(found[k])
        else:
            real, imag = found[order - k]
            packed.append((real, -imag))
    out = complex_fft(packed, -1)
    out = [turn(out[n], -n, order) for n in range(quarter)]
    return [value[0] for value in out] + [-value[1] for value in out]


def real_inverse(found, size):
    if size == 2:
        return [found[0][0] + found[1][0], found[0][0] - found[1][0]]
    half = size // 2
    evens = real_inverse({k // 2: value for k, value in found.items() if k % 2 == 0}, half)
    odds = odd_inverse(found, size)
    return [evens[n] + odds[n] for n in range(half)] + [evens[n] - odds[n] for n in range(half)]


def padded_inverse(found):
    evens = real_inverse({k // 2: value for k, value in found.items() if k % 2 == 0}, HALF)
    odds = odd_inverse(found, RADIX)
    return [evens[n] + odds[n] for n in range(HALF)]


def tables():
    k = np.arange(LANES)
    angles = 2.0 * np.pi * (k[:, None] * k[None, :] % LANES) / LANES
    cos, sin = np.cos(angles), np.sin(angles)
    forward = np.block([[cos, -sin], [sin, cos]])
    inverse = forward.T

    def split(matrix):
        high = matrix.astype(np.float32).astype(jnp.bfloat16)
        low = (matrix - high.astype(np.float64)).astype(np.float32).astype(jnp.bfloat16)
        return high, low

    matrices = np.stack([*split(forward), *split(inverse)])
    length = RADIX * LANES
    first = np.arange(KEPT)
    angles = 2.0 * np.pi * (first[:, None] * k[None, :]) / length
    scale = np.where((first == 0) | (first == HALF), 1.0, 2.0)[:, None] / length
    twists = np.stack(
        [np.cos(angles), np.sin(angles), np.cos(angles) * scale, np.sin(angles) * scale]
    ).astype(np.float32)
    return matrices, twists


CHUNKS = 2


def body(
    ctx,
    dp,
    q_ref,
    k_ref,
    v_ref,
    g_ref,
    f_ref,
    w_ref,
    t_ref,
    out_ref,
    gq_ref,
    gk_ref,
    gv_ref,
    gf_ref,
    send_x,
    recv_x,
    send_y,
    recv_y,
    part_g,
    recv_g,
    own_g,
    swap_g,
    spec_a,
    spec_b,
    sx_send,
    sx_recv,
    sf_send,
    sf_recv,
    sy_send,
    sy_recv,
    sg_send,
    sg_recv,
    sp_send,
    sp_recv,
    sa_send,
    sa_recv,
):
    me_c = lax.axis_index("ctx")
    me_d = lax.axis_index("dp")
    share = q_ref.shape[0] // ctx
    rows = share // CHUNKS
    subs = rows // 8
    width = q_ref.shape[1]

    barrier = pltpu.get_barrier_semaphore()

    def greet_ctx(i, carry):
        pl.semaphore_signal(
            barrier, inc=1, device_id=(me_d, (me_c + i) % ctx), device_id_type=MESH
        )
        return carry

    def greet_dp(i, carry):
        pl.semaphore_signal(
            barrier, inc=1, device_id=((me_d + i) % dp, me_c), device_id_type=MESH
        )
        return carry

    lax.fori_loop(1, ctx, greet_ctx, 0)
    lax.fori_loop(1, dp, greet_dp, 0)

    @pl.when(me_c != me_d)
    def _():
        pl.semaphore_signal(barrier, inc=1, device_id=(me_c, me_d), device_id_type=MESH)

    def products(b, carry):
        for ck in range(CHUNKS):
            at = pl.ds(b * share + ck * rows, rows)
            send_x[ck, 0, b] = k_ref[at, :].astype(jnp.float32) * v_ref[at, :].astype(jnp.float32)
            send_x[ck, 1, b] = q_ref[at, :].astype(jnp.float32) * g_ref[at, :].astype(jnp.float32)
        return carry

    lax.fori_loop(0, ctx, products, 0)
    for ck in range(CHUNKS):
        recv_x[ck, 0, me_c] = send_x[ck, 0, me_c]
        recv_x[ck, 1, me_c] = send_x[ck, 1, me_c]
        recv_x[ck, 2, me_c] = f_ref[pl.ds(me_c * share + ck * rows, rows), :]

    @pl.when(me_c != me_d)
    def _():
        pl.semaphore_wait(barrier, ctx + dp - 1)

    @pl.when(me_c == me_d)
    def _():
        pl.semaphore_wait(barrier, ctx + dp - 2)

    def copy_x(ck, i):
        peer = (me_c + i) % ctx
        return pltpu.make_async_remote_copy(
            src_ref=send_x.at[ck, :, peer],
            dst_ref=recv_x.at[ck, pl.ds(0, 2), me_c],
            send_sem=sx_send.at[ck, i],
            recv_sem=sx_recv.at[ck, i],
            device_id=(me_d, peer),
            device_id_type=MESH,
        )

    def copy_f(ck, i):
        peer = (me_c + i) % ctx
        return pltpu.make_async_remote_copy(
            src_ref=f_ref.at[pl.ds(peer * share + ck * rows, rows), :],
            dst_ref=recv_x.at[ck, 2, me_c],
            send_sem=sf_send.at[ck, i],
            recv_sem=sf_recv.at[ck, i],
            device_id=(me_d, peer),
            device_id_type=MESH,
        )

    def copy_y(ck, i):
        peer = (me_c + i) % ctx
        return pltpu.make_async_remote_copy(
            src_ref=send_y.at[ck, :, peer],
            dst_ref=recv_y.at[ck, :, me_c],
            send_sem=sy_send.at[ck, i],
            recv_sem=sy_recv.at[ck, i],
            device_id=(me_d, peer),
            device_id_type=MESH,
        )

    def copy_g(ck, i):
        peer = (me_d + i) % dp
        return pltpu.make_async_remote_copy(
            src_ref=part_g.at[ck, peer],
            dst_ref=recv_g.at[ck, i],
            send_sem=sg_send.at[ck, i],
            recv_sem=sg_recv.at[ck, i],
            device_id=(peer, me_c),
            device_id_type=MESH,
        )

    def copy_a(i):
        peer = (me_d + i) % dp
        return pltpu.make_async_remote_copy(
            src_ref=swap_g,
            dst_ref=gf_ref.at[me_d],
            send_sem=sa_send.at[i],
            recv_sem=sa_recv.at[i],
            device_id=(peer, me_c),
            device_id_type=MESH,
        )

    swap = pltpu.make_async_remote_copy(
        src_ref=own_g,
        dst_ref=swap_g,
        send_sem=sp_send.at[0],
        recv_sem=sp_recv.at[0],
        device_id=(me_c, me_d),
        device_id_type=MESH,
    )

    def each(count, act):
        def step(i, carry):
            act(i)
            return carry

        lax.fori_loop(1, count, step, 0)

    for ck in range(CHUNKS):
        each(ctx, lambda i: copy_x(ck, i).start())
        each(ctx, lambda i: copy_f(ck, i).start())

    def matmul(sig, which):
        data = spec_a[sig]
        high = data.astype(jnp.bfloat16)
        low = (data - high.astype(jnp.float32)).astype(jnp.bfloat16)
        w_high = w_ref[2 * which]
        w_low = w_ref[2 * which + 1]
        spec_b[sig] = (
            jnp.dot(high, w_high, preferred_element_type=jnp.float32)
            + jnp.dot(low, w_high, preferred_element_type=jnp.float32)
            + jnp.dot(high, w_low, preferred_element_type=jnp.float32)
        )

    def chunk(ck):
        each(ctx, lambda i: copy_x(ck, i).wait_recv())
        each(ctx, lambda i: copy_f(ck, i).wait_recv())

        def forward(step, carry):
            sig, sub = step // subs, step % subs
            at = pl.ds(sub * 8, 8)
            values = [
                recv_x[ck, sig, n // 2, at, pl.ds((n % 2) * LANES, LANES)] for n in range(HALF)
            ]
            found = padded_forward(values)
            for k in range(KEPT):
                cos, sin = t_ref[0, pl.ds(k, 1), :], t_ref[1, pl.ds(k, 1), :]
                real, imag = found[k]
                to = pl.ds(k * rows + sub * 8, 8)
                if k == 0:
                    spec_a[sig, to, pl.ds(0, LANES)] = real
                    spec_a[sig, to, pl.ds(LANES, LANES)] = jnp.zeros_like(real)
                elif imag is None:
                    spec_a[sig, to, pl.ds(0, LANES)] = real * cos
                    spec_a[sig, to, pl.ds(LANES, LANES)] = -(real * sin)
                else:
                    spec_a[sig, to, pl.ds(0, LANES)] = real * cos + imag * sin
                    spec_a[sig, to, pl.ds(LANES, LANES)] = imag * cos - real * sin
            return carry

        lax.fori_loop(0, 3 * subs, forward, 0)
        lax.fori_loop(0, 3, lambda sig, carry: (matmul(sig, 0), carry)[1], 0)

        def pointwise(k, carry):
            at = pl.ds(k * rows, rows)
            re, im = pl.ds(0, LANES), pl.ds(LANES, LANES)
            z_re, z_im = spec_b[0, at, re], spec_b[0, at, im]
            d_re, d_im = spec_b[1, at, re], spec_b[1, at, im]
            f_re, f_im = spec_b[2, at, re], spec_b[2, at, im]
            spec_a[0, at, re] = z_re * f_re - z_im * f_im
            spec_a[0, at, im] = z_re * f_im + z_im * f_re
            spec_a[1, at, re] = f_re * d_re + f_im * d_im
            spec_a[1, at, im] = f_re * d_im - f_im * d_re
            spec_a[2, at, re] = z_re * d_re + z_im * d_im
            spec_a[2, at, im] = z_re * d_im - z_im * d_re
            return carry

        lax.fori_loop(0, KEPT, pointwise, 0)
        lax.fori_loop(0, 3, lambda sig, carry: (matmul(sig, 1), carry)[1], 0)

        def inverse(sig, sub, store):
            found = {}
            for k in range(KEPT):
                cos, sin = t_ref[2, pl.ds(k, 1), :], t_ref[3, pl.ds(k, 1), :]
                at = pl.ds(k * rows + sub * 8, 8)
                real = spec_b[sig, at, pl.ds(0, LANES)]
                imag = spec_b[sig, at, pl.ds(LANES, LANES)]
                if k == 0 or k == HALF:
                    found[k] = (real * cos - imag * sin, None)
                else:
                    found[k] = (real * cos - imag * sin, imag * cos + real * sin)
            values = padded_inverse(found)
            for n in range(HALF):
                store(n // 2, pl.ds(sub * 8, 8), pl.ds((n % 2) * LANES, LANES), values[n])

        def back_y(step, carry):
            sig, sub = step // subs, step % subs

            def store(block, at, lanes, value):
                send_y[ck, sig, block, at, lanes] = value

            inverse(sig, sub, store)
            return carry

        def back_g(sub, carry):
            def store(block, at, lanes, value):
                part_g[ck, block, at, lanes] = value

            inverse(2, sub, store)
            return carry

        lax.fori_loop(0, subs, back_g, 0)
        each(dp, lambda i: copy_g(ck, i).start())
        lax.fori_loop(0, 2 * subs, back_y, 0)
        each(ctx, lambda i: copy_y(ck, i).start())
        recv_y[ck, 0, me_c] = send_y[ck, 0, me_c]
        recv_y[ck, 1, me_c] = send_y[ck, 1, me_c]

    for ck in range(CHUNKS):
        chunk(ck)

    scale = 1.0 / math.sqrt(dp * ctx * width)
    for ck in range(CHUNKS):
        each(dp, lambda i: copy_g(ck, i).wait_recv())
        total = part_g[ck, me_d]
        for i in range(1, dp):
            total = total + recv_g[ck, i]
        own_g[pl.ds(ck * rows, rows), :] = total * scale

    @pl.when(me_c != me_d)
    def _():
        swap.start()
        swap.wait()

    @pl.when(me_c == me_d)
    def _():
        swap_g[...] = own_g[...]

    each(dp, lambda i: copy_a(i).start())
    gf_ref[me_d] = swap_g[...]

    for ck in range(CHUNKS):
        each(ctx, lambda i: copy_y(ck, i).wait_recv())

        def outputs(b, carry):
            at = pl.ds(b * share + ck * rows, rows)
            conv = recv_y[ck, 0, b]
            dmixed = recv_y[ck, 1, b]
            out_ref[at, :] = (q_ref[at, :].astype(jnp.float32) * conv).astype(jnp.bfloat16)
            gq_ref[at, :] = (g_ref[at, :].astype(jnp.float32) * conv).astype(jnp.bfloat16)
            gk_ref[at, :] = (v_ref[at, :].astype(jnp.float32) * dmixed).astype(jnp.bfloat16)
            gv_ref[at, :] = (k_ref[at, :].astype(jnp.float32) * dmixed).astype(jnp.bfloat16)
            return carry

        lax.fori_loop(0, ctx, outputs, 0)

    each(dp, lambda i: copy_a(i).wait_recv())
    for ck in range(CHUNKS):
        each(ctx, lambda i: copy_x(ck, i).wait_send())
        each(ctx, lambda i: copy_f(ck, i).wait_send())
        each(ctx, lambda i: copy_y(ck, i).wait_send())
        each(dp, lambda i: copy_g(ck, i).wait_send())
    each(dp, lambda i: copy_a(i).wait_send())


def shards(ctx, dp, query, key_act, value_act, filter_taps, grad_out):
    _, channels, width = query.shape
    share = channels // ctx
    rows = share // CHUNKS
    matrices, twists = tables()
    vmem = pl.BlockSpec(memory_space=pltpu.VMEM)
    half = jax.ShapeDtypeStruct((channels, width), jnp.bfloat16)
    dma = pltpu.SemaphoreType.DMA
    outs = pl.pallas_call(
        functools.partial(body, ctx, dp),
        out_shape=[half] * 4 + [jax.ShapeDtypeStruct((dp, share, width), jnp.float32)],
        in_specs=[vmem] * 7,
        out_specs=[vmem] * 5,
        scratch_shapes=[
            pltpu.VMEM((CHUNKS, 2, ctx, rows, width), jnp.float32),
            pltpu.VMEM((CHUNKS, 3, ctx, rows, width), jnp.float32),
            pltpu.VMEM((CHUNKS, 2, ctx, rows, width), jnp.float32),
            pltpu.VMEM((CHUNKS, 2, ctx, rows, width), jnp.float32),
            pltpu.VMEM((CHUNKS, ctx, rows, width), jnp.float32),
            pltpu.VMEM((CHUNKS, dp, rows, width), jnp.float32),
            pltpu.VMEM((share, width), jnp.float32),
            pltpu.VMEM((share, width), jnp.float32),
            pltpu.VMEM((3, KEPT * rows, 2 * LANES), jnp.float32),
            pltpu.VMEM((3, KEPT * rows, 2 * LANES), jnp.float32),
            dma((CHUNKS, ctx)),
            dma((CHUNKS, ctx)),
            dma((CHUNKS, ctx)),
            dma((CHUNKS, ctx)),
            dma((CHUNKS, ctx)),
            dma((CHUNKS, ctx)),
            dma((CHUNKS, dp)),
            dma((CHUNKS, dp)),
            dma((1,)),
            dma((1,)),
            dma((dp,)),
            dma((dp,)),
        ],
        compiler_params=pltpu.CompilerParams(
            collective_id=0, has_side_effects=True, vmem_limit_bytes=40 * 1024 * 1024
        ),
        cost_estimate=pl.CostEstimate(
            flops=3 * 2 * 6 * KEPT * share * 256 * 256, bytes_accessed=4 * 2**20, transcendentals=0
        ),
    )(
        query.reshape(channels, width),
        key_act.reshape(channels, width),
        value_act.reshape(channels, width),
        grad_out.reshape(channels, width),
        filter_taps,
        jnp.asarray(matrices),
        jnp.asarray(twists),
    )
    shape = query.shape
    return (
        outs[0].reshape(shape),
        outs[1].reshape(shape),
        outs[2].reshape(shape),
        outs[3].reshape(shape),
        outs[4].reshape(channels, width),
    )


def solution(mesh):
    row = P("dp", None, "ctx")
    taps = P(None, "ctx")
    return jax.shard_map(
        functools.partial(shards, mesh.shape["ctx"], mesh.shape["dp"]),
        mesh=mesh,
        in_specs=(row, row, row, taps, row),
        out_specs=(row, row, row, row, taps),
        check_vma=False,
    )
```

time: 963 us -> 79.7 us (0.08)
  waiting for transfers between devices: 668 us -> 0 us
  matrix products: 80.4 us -> 0 us
  Pallas kernels: 0 us -> 68.1 us
  starting transfers between devices: 68 us -> 0 us
  local copies, waits for them, and re-layouts: 70.9 us -> 10.4 us
  blocking collectives: 41.6 us -> 0 us
  between operations: 15 us -> 0.66 us
  other arithmetic: 11.5 us -> 0 us
    unnamed x6 -> x0, waiting for transfers between devices: 369 us -> none
    all_gather x2 -> x0, waiting for transfers between devices: 205 us -> none  [the longest x1 129 us: shards(): lax.all_gather(stacked_imag[rows_count:], 'dp', axis=0, tiled=True)]
    all_to_all x12 -> x0, waiting for transfers between devices: 94 us -> none  [the longest x2 28.1 us: forward_spectrum(): lax.all_to_all(imag_part, 'ctx', split_axis=1, concat_axis=2, tiled=True)]
    dot_general x40 -> x0, matrix products: 80.4 us -> none  [the longest x2 8.95 us: forward_spectrum(): jnp.einsum('rjab,bk->rjak', turned_real, second_sin, precision=PRECISE)]
    pallas_call x0 -> x1, Pallas kernels: none -> 68.1 us  [shards(): pl.pallas_call(functools.partial(body, ctx, dp), out_shape=[half] * 4 + [...]
    all_to_all x12 -> x0, starting transfers between devices: 67.4 us -> none  [the longest x2 12.7 us: forward_spectrum(): lax.all_to_all(real_part, 'ctx', split_axis=1, concat_axis=2, tiled=True)]
    all_gather x1 -> x0, blocking collectives: 41.6 us -> none  [shards(): lax.all_gather(inverted[rows_count:] * scale, 'dp', axis=0, tiled=True)]
    all_to_all x12 -> x0, local copies, waits for them, and re-layouts: 17.1 us -> none  [the longest x6 8.64 us: inverse_spectrum(): lax.all_to_all(time_real, 'ctx', split_axis=2, concat_axis=1, tiled=True)]
  transfers between devices with their start and end apart: 16 -> 0, of which waited for: 15 -> 0; matrix products, arithmetic and copies ran while one was open for 12% -> 0% of each run, Pallas kernels for 0% -> 0%
where the time goes in v1:
time: 79.7 us; the launch traced here: 79.1 us
  Pallas kernels  68.1 us (85%)
  local copies, waits for them, and re-layouts  10.4 us (13%)
    pallas_call x1, Pallas kernels, shards(): pl.pallas_call(functools.partial(body, ctx, dp), out_shape=[half] * 4 + [...  68.1 us
    unnamed x19, local copies, waits for them, and re-layouts  10.4 us

profile of v1, /device:TPU:6, one launch (start us, length us, event | category | flops | bytes accessed | tf_op | source)
XLA Modules:
  0.0 79.1 jit_solution(17217465660996223797)
XLA Ops:
  0.6 0.0 copy-start
  0.6 1.0 %copy-done = f32[512,256]{1,0:T(8,128)S(1)} copy-done((f32[512,256]{1,0:T(8,128)S(1)}, f32[512,256]{1,0:T(8,128)}, u32[]{:S(2)}) %copy-start) | copy-done | bytes 524312
  1.7 0.0 copy-start.1
  1.7 0.9 %copy-done.1 = bf16[1,512,256]{2,1,0:T(8,128)(2,1)S(1)} copy-done((bf16[1,512,256]{2,1,0:T(8,128)(2,1)S(1)}, bf16[1,512,256]{2,1,0:T(8,128)(2,1)}, u32[]{:S(2)}) %copy-start.1) | copy-done | bytes 262168
  2.6 0.0 copy-start.2
  2.6 0.9 %copy-done.2 = bf16[1,512,256]{2,1,0:T(8,128)(2,1)S(1)} copy-done((bf16[1,512,256]{2,1,0:T(8,128)(2,1)S(1)}, bf16[1,512,256]{2,1,0:T(8,128)(2,1)}, u32[]{:S(2)}) %copy-start.2) | copy-done | bytes 262168
  3.6 0.0 copy-start.3
  3.6 0.9 %copy-done.3 = bf16[1,512,256]{2,1,0:T(8,128)(2,1)S(1)} copy-done((bf16[1,512,256]{2,1,0:T(8,128)(2,1)S(1)}, bf16[1,512,256]{2,1,0:T(8,128)(2,1)}, u32[]{:S(2)}) %copy-start.3) | copy-done | bytes 262168
  4.5 0.0 copy-start.4
  4.5 0.9 %copy-done.4 = bf16[1,512,256]{2,1,0:T(8,128)(2,1)S(1)} copy-done((bf16[1,512,256]{2,1,0:T(8,128)(2,1)S(1)}, bf16[1,512,256]{2,1,0:T(8,128)(2,1)}, u32[]{:S(2)}) %copy-start.4) | copy-done | bytes 262168
  5.5 0.0 copy-start.5
  5.5 1.0 %copy-done.5 = bf16[4,256,256]{2,1,0:T(8,128)(2,1)S(1)} copy-done((bf16[4,256,256]{2,1,0:T(8,128)(2,1)S(1)}, bf16[4,256,256]{2,1,0:T(8,128)(2,1)}, u32[]{:S(2)}) %copy-start.5) | copy-done | bytes 524312
  6.5 0.0 copy-start.6
  6.5 0.9 %copy-done.6 = f32[4,33,128]{2,1,0:T(8,128)S(1)} copy-done((f32[4,33,128]{2,1,0:T(8,128)S(1)}, f32[4,33,128]{2,1,0:T(8,128)}, u32[]{:S(2)}) %copy-start.6) | copy-done | bytes 67608
  7.4 68.1 %shard_map.110 = (bf16[512,256]{1,0:T(8,128)(2,1)S(1)}, bf16[512,256]{1,0:T(8,128)(2,1)S(1)}, bf16[512,256]{1,0:T(8,128)(2,1)S(1)}, bf16[512,256]{1,0:T(8,128)(2,1)S(1)}, f32[16,32,256]{2,1,0:T(8,128)S(1)}) custom-call(bf16[512,256]{1,0:T(8,128)(2,1)S(1)} %bitcast.14, bf16[512,256]{1,0:T(8,128)(2,1)S(1)} %bitcast.15, bf16[512,256]{1,0:T(8,128)(2,1)S(1)} %bitcast.16, ...), custom_call_target="tpu_custom_call" | custom-call | flops 2491416576 | bytes 4194304 | tf_op jit(solution)/shard_map/pallas_call | solution.py:461
  75.5 0.7 copy.17
  76.2 0.7 copy.18
  76.9 0.7 copy.19
  77.6 0.7 copy.20
  78.3 0.8 %copy.21 = f32[512,256]{1,0:T(8,128)} copy(f32[512,256]{1,0:T(8,128)S(1)} %bitcast.9) | data formatting | bytes 1048576
Async XLA Ops:
  0.6 1.0 %copy-start = (f32[512,256]{1,0:T(8,128)S(1)}, f32[512,256]{1,0:T(8,128)}, u32[]{:S(2)}) copy-start(f32[512,256]{1,0:T(8,128)} %f_ref.1) | copy-start | bytes 1572868
  1.7 0.9 %copy-start.1 = (bf16[1,512,256]{2,1,0:T(8,128)(2,1)S(1)}, bf16[1,512,256]{2,1,0:T(8,128)(2,1)}, u32[]{:S(2)}) copy-start(bf16[1,512,256]{2,1,0:T(8,128)(2,1)} %param.7) | copy-start | bytes 786436
  2.6 0.9 %copy-start.2 = (bf16[1,512,256]{2,1,0:T(8,128)(2,1)S(1)}, bf16[1,512,256]{2,1,0:T(8,128)(2,1)}, u32[]{:S(2)}) copy-start(bf16[1,512,256]{2,1,0:T(8,128)(2,1)} %param.8) | copy-start | bytes 786436
  3.6 0.9 %copy-start.3 = (bf16[1,512,256]{2,1,0:T(8,128)(2,1)S(1)}, bf16[1,512,256]{2,1,0:T(8,128)(2,1)}, u32[]{:S(2)}) copy-start(bf16[1,512,256]{2,1,0:T(8,128)(2,1)} %param.9) | copy-start | bytes 786436
  4.5 0.9 %copy-start.4 = (bf16[1,512,256]{2,1,0:T(8,128)(2,1)S(1)}, bf16[1,512,256]{2,1,0:T(8,128)(2,1)}, u32[]{:S(2)}) copy-start(bf16[1,512,256]{2,1,0:T(8,128)(2,1)} %param.11) | copy-start | bytes 786436
  5.5 1.0 %copy-start.5 = (bf16[4,256,256]{2,1,0:T(8,128)(2,1)S(1)}, bf16[4,256,256]{2,1,0:T(8,128)(2,1)}, u32[]{:S(2)}) copy-start(bf16[4,256,256]{2,1,0:T(8,128)(2,1)} %constant.4.clone.w_ref) | copy-start | bytes 1572868
  6.5 0.9 %copy-start.6 = (f32[4,33,128]{2,1,0:T(8,128)S(1)}, f32[4,33,128]{2,1,0:T(8,128)}, u32[]{:S(2)}) copy-start(f32[4,33,128]{2,1,0:T(8,128)} %constant.5.clone.t_ref) | copy-start | bytes 202756

commit v2 on v1

v2 whole, which is shorter than its diff:
```python
import functools
import math

import jax
import jax.numpy as jnp
import numpy as np
from jax import lax
from jax.experimental import pallas as pl
from jax.experimental.pallas import tpu as pltpu
from jax.sharding import PartitionSpec as P

MESH = pl.DeviceIdType.MESH
LANES = 128
RADIX = 64
HALF = RADIX // 2
KEPT = HALF + 1


def turn(value, numerator, denominator):
    real, imag = value
    numerator %= denominator
    eighth = numerator * 8
    if eighth % denominator == 0:
        step = eighth // denominator
        if step == 0:
            return (real, imag)
        if step == 2:
            return (imag, -real)
        if step == 4:
            return (-real, -imag)
        if step == 6:
            return (-imag, real)
        root = math.sqrt(0.5)
        if step == 1:
            return ((real + imag) * root, (imag - real) * root)
        if step == 3:
            return ((imag - real) * root, (real + imag) * -root)
        if step == 5:
            return ((real + imag) * -root, (real - imag) * root)
        return ((real - imag) * root, (real + imag) * root)
    cos = math.cos(2.0 * math.pi * numerator / denominator)
    sin = math.sin(2.0 * math.pi * numerator / denominator)
    return (real * cos + imag * sin, imag * cos - real * sin)


def complex_fft(values, sign):
    size = len(values)
    if size == 1:
        return values
    even = complex_fft(values[0::2], sign)
    odd = complex_fft(values[1::2], sign)
    low, high = [], []
    for k in range(size // 2):
        real, imag = turn(odd[k], sign * k, size)
        low.append((even[k][0] + real, even[k][1] + imag))
        high.append((even[k][0] - real, even[k][1] - imag))
    return low + high


def odd_forward(values):
    quarter = len(values) // 2
    order = 4 * quarter
    packed = [turn((values[n], -values[n + quarter]), n, order) for n in range(quarter)]
    out = complex_fft(packed, 1)
    found = {}
    for j in range(quarter):
        k = 4 * j + 1
        if k < order // 2:
            found[k] = out[j]
        else:
            found[order - k] = (out[j][0], -out[j][1])
    return found


def real_forward(values):
    size = len(values)
    if size == 2:
        return {0: (values[0] + values[1], None), 1: (values[0] - values[1], None)}
    half = size // 2
    evens = real_forward([values[n] + values[n + half] for n in range(half)])
    found = {2 * k: value for k, value in evens.items()}
    found.update(odd_forward([values[n] - values[n + half] for n in range(half)]))
    return found


def padded_forward(values):
    found = {2 * k: value for k, value in real_forward(values).items()}
    found.update(odd_forward(values))
    return found


def odd_inverse(found, order):
    quarter = order // 4
    packed = []
    for j in range(quarter):
        k = 4 * j + 1
        if k < order // 2:
            packed.append(found[k])
        else:
            real, imag = found[order - k]
            packed.append((real, -imag))
    out = complex_fft(packed, -1)
    out = [turn(out[n], -n, order) for n in range(quarter)]
    return [value[0] for value in out] + [-value[1] for value in out]


def real_inverse(found, size):
    if size == 2:
        return [found[0][0] + found[1][0], found[0][0] - found[1][0]]
    half = size // 2
    evens = real_inverse({k // 2: value for k, value in found.items() if k % 2 == 0}, half)
    odds = odd_inverse(found, size)
    return [evens[n] + odds[n] for n in range(half)] + [evens[n] - odds[n] for n in range(half)]


def padded_inverse(found):
    evens = real_inverse({k // 2: value for k, value in found.items() if k % 2 == 0}, HALF)
    odds = odd_inverse(found, RADIX)
    return [evens[n] + odds[n] for n in range(HALF)]


def tables():
    k = np.arange(LANES)
    angles = 2.0 * np.pi * (k[:, None] * k[None, :] % LANES) / LANES
    cos, sin = np.cos(angles), np.sin(angles)
    forward = np.block([[cos, -sin], [sin, cos]])
    inverse = forward.T

    def split(matrix):
        high = matrix.astype(np.float32).astype(jnp.bfloat16)
        low = (matrix - high.astype(np.float64)).astype(np.float32).astype(jnp.bfloat16)
        return high, low

    matrices = np.stack([*split(forward), *split(inverse)])
    length = RADIX * LANES
    first = np.arange(KEPT)
    angles = 2.0 * np.pi * (first[:, None] * k[None, :]) / length
    scale = np.where((first == 0) | (first == HALF), 1.0, 2.0)[:, None] / length
    twists = np.stack(
        [np.cos(angles), np.sin(angles), np.cos(angles) * scale, np.sin(angles) * scale]
    ).astype(np.float32)
    return matrices, twists


CHUNKS = 2
PLANES = 2
GRANT = 60 * 1024 * 1024


def body(
    ctx,
    dp,
    q_hbm,
    k_hbm,
    v_hbm,
    g_hbm,
    f_hbm,
    w_hbm,
    t_hbm,
    out_hbm,
    gq_hbm,
    gk_hbm,
    gv_hbm,
    gf_ref,
    out_ref,
    gq_ref,
    gk_ref,
    gv_ref,
    q_ref,
    k_ref,
    v_ref,
    g_ref,
    w_ref,
    t_ref,
    send_x,
    recv_x,
    send_y,
    recv_y,
    part_g,
    recv_g,
    sum_g,
    recv_s,
    own_s,
    spec_a,
    spec_b,
    load_sem,
    save_sem,
    own_sem,
    keep_sem,
    sx_send,
    sx_recv,
    sf_send,
    sf_recv,
    sy_send,
    sy_recv,
    sg_send,
    sg_recv,
    ss_send,
    ss_recv,
    sa_send,
    sa_recv,
):
    me_c = lax.axis_index("ctx")
    me_d = lax.axis_index("dp")
    ring = dp // PLANES
    channels, width = q_ref.shape
    share = channels // ctx
    rows = share // CHUNKS
    subs = rows // 8
    me_p, me_z = me_d // ring, lax.rem(me_d, ring)
    c_p, c_z = me_c // ring, lax.rem(me_c, ring)

    loads = [
        pltpu.make_async_copy(src, dst, load_sem.at[n])
        for n, (src, dst) in enumerate(
            [
                (k_hbm, k_ref),
                (v_hbm, v_ref),
                (q_hbm, q_ref),
                (g_hbm, g_ref),
                (w_hbm, w_ref),
                (t_hbm, t_ref),
            ]
        )
    ]
    for load in loads:
        load.start()

    def each(first, last, act):
        def step(i, carry):
            act(i)
            return carry

        lax.fori_loop(first, last, step, 0, unroll=True)

    def ctx_peer(i):
        return (me_d, lax.rem(me_c + i, ctx))

    def ring_peer(i):
        return (me_p * ring + lax.rem(me_z + i, ring), me_c)

    def swap_peer(plane, part):
        return (plane * ring + c_z, part * ring + me_z)

    def is_self(plane, part):
        return (c_z == me_z) & (plane == me_p) & (part == c_p)

    barrier = pltpu.get_barrier_semaphore()

    def greet(peer):
        pl.semaphore_signal(barrier, inc=1, device_id=peer, device_id_type=MESH)

    each(1, ctx, lambda i: greet(ctx_peer(i)))
    each(1, ring, lambda i: greet(ring_peer(i)))
    swaps = [(plane, part) for plane in range(PLANES) for part in range(PLANES)]
    for plane, part in swaps:
        pl.when(jnp.logical_not(is_self(plane, part)))(
            functools.partial(greet, swap_peer(plane, part))
        )

    for load in loads[:4]:
        load.wait()

    def products(b, carry):
        at = pl.ds(b * share, share)
        mixed = k_ref[at, :].astype(jnp.float32) * v_ref[at, :].astype(jnp.float32)
        dconv = q_ref[at, :].astype(jnp.float32) * g_ref[at, :].astype(jnp.float32)
        for ck in range(CHUNKS):
            send_x[ck, 0, b] = mixed[ck * rows : (ck + 1) * rows]
            send_x[ck, 1, b] = dconv[ck * rows : (ck + 1) * rows]
        return carry

    lax.fori_loop(0, ctx, products, 0)

    met = ctx - 1 + ring - 1 + len(swaps)

    @pl.when(c_z == me_z)
    def _():
        pl.semaphore_wait(barrier, met - 1)

    @pl.when(c_z != me_z)
    def _():
        pl.semaphore_wait(barrier, met)

    def remote(src, dst, send, recv, peer):
        return pltpu.make_async_remote_copy(
            src_ref=src,
            dst_ref=dst,
            send_sem=send,
            recv_sem=recv,
            device_id=peer,
            device_id_type=MESH,
        )

    def copy_x(ck, i):
        peer = ctx_peer(i)
        return remote(
            send_x.at[ck, :, peer[1]],
            recv_x.at[ck, pl.ds(0, 2), me_c],
            sx_send.at[ck],
            sx_recv.at[ck],
            peer,
        )

    def copy_f(ck, i):
        peer = ctx_peer(i)
        return remote(
            f_hbm.at[pl.ds(peer[1] * share + ck * rows, rows), :],
            recv_x.at[ck, 2, me_c],
            sf_send.at[ck],
            sf_recv.at[ck],
            peer,
        )

    def own_f(ck):
        return pltpu.make_async_copy(
            f_hbm.at[pl.ds(me_c * share + ck * rows, rows), :],
            recv_x.at[ck, 2, me_c],
            own_sem.at[ck],
        )

    def copy_y(ck, i):
        peer = ctx_peer(i)
        return remote(
            send_y.at[ck, :, peer[1]],
            recv_y.at[ck, :, me_c],
            sy_send.at[ck],
            sy_recv.at[ck],
            peer,
        )

    def copy_g(ck, i):
        peer = ring_peer(i)
        return remote(
            part_g.at[ck, :, lax.rem(me_z + i, ring)],
            recv_g.at[ck, i - 1],
            sg_send.at[ck],
            sg_recv.at[ck],
            peer,
        )

    def copy_s(ck, plane, part):
        return remote(
            sum_g.at[ck, part],
            recv_s.at[ck, c_p, me_p],
            ss_send.at[ck, plane, part],
            ss_recv.at[ck, c_p, me_p],
            swap_peer(plane, part),
        )

    def copy_a(ck, i):
        return remote(
            own_s.at[ck],
            gf_ref.at[:, me_z, ck],
            sa_send.at[ck],
            sa_recv.at[ck],
            ring_peer(i),
        )

    def keep(ck):
        return pltpu.make_async_copy(own_s.at[ck], gf_ref.at[:, me_z, ck], keep_sem.at[ck])

    def drain(ref, sem):
        pltpu.make_async_copy(ref, ref, sem).wait()

    def chunks(act):
        def step(ck, carry):
            act(ck)
            return carry

        lax.fori_loop(0, CHUNKS, step, 0)

    chunks(lambda ck: each(1, ctx, lambda i: copy_x(ck, i).start()))

    def first_f(ck):
        each(1, ctx, lambda i: copy_f(ck, i).start())
        own_f(ck).start()

    chunks(first_f)

    def own_x(ck):
        recv_x[ck, 0, me_c] = send_x[ck, 0, me_c]
        recv_x[ck, 1, me_c] = send_x[ck, 1, me_c]

    chunks(own_x)
    for load in loads[4:]:
        load.wait()

    re, im = pl.ds(0, LANES), pl.ds(LANES, LANES)

    def forward(ck, sig, sub):
        at = pl.ds(sub * 8, 8)
        values = [
            recv_x[ck, sig, n // 2, at, pl.ds((n % 2) * LANES, LANES)] for n in range(HALF)
        ]
        found = padded_forward(values)
        for k in range(KEPT):
            cos, sin = t_ref[0, pl.ds(k, 1), :], t_ref[1, pl.ds(k, 1), :]
            real, imag = found[k]
            to = pl.ds(k * rows + sub * 8, 8)
            if k == 0:
                spec_a[sig, to, re] = real
                spec_a[sig, to, im] = jnp.zeros_like(real)
            elif imag is None:
                spec_a[sig, to, re] = real * cos
                spec_a[sig, to, im] = -(real * sin)
            else:
                spec_a[sig, to, re] = real * cos + imag * sin
                spec_a[sig, to, im] = imag * cos - real * sin

    def inverse(ck, sig, sub, store):
        found = {}
        for k in range(KEPT):
            cos, sin = t_ref[2, pl.ds(k, 1), :], t_ref[3, pl.ds(k, 1), :]
            at = pl.ds(k * rows + sub * 8, 8)
            real = spec_a[sig, at, re]
            imag = spec_a[sig, at, im]
            if k == 0 or k == HALF:
                found[k] = (real * cos - imag * sin, None)
            else:
                found[k] = (real * cos - imag * sin, imag * cos + real * sin)
        values = padded_inverse(found)
        for n in range(HALF):
            store(n // 2, pl.ds(sub * 8, 8), pl.ds((n % 2) * LANES, LANES), values[n])

    def matmul(src, dst, which):
        data = src[...]
        high = data.astype(jnp.bfloat16)
        low = (data - high.astype(jnp.float32)).astype(jnp.bfloat16)
        w_high = w_ref[2 * which]
        w_low = w_ref[2 * which + 1]
        dst[...] = (
            jnp.dot(high, w_high, preferred_element_type=jnp.float32)
            + jnp.dot(low, w_high, preferred_element_type=jnp.float32)
            + jnp.dot(high, w_low, preferred_element_type=jnp.float32)
        )

    def loop(count, act, unroll=1):
        def step(i, carry):
            act(i)
            return carry

        lax.fori_loop(0, count, step, 0, unroll=unroll)

    def filter_grad(ck):
        drain(recv_x.at[ck, pl.ds(0, 2), pl.ds(0, ctx - 1)], sx_recv.at[ck])
        loop(2 * subs, lambda n: forward(ck, n // subs, lax.rem(n, subs)))
        loop(2, lambda sig: matmul(spec_a.at[sig], spec_b.at[ck, sig], 0))

        def pointwise(k):
            at = pl.ds(k * rows, rows)
            z_re, z_im = spec_b[ck, 0, at, re], spec_b[ck, 0, at, im]
            d_re, d_im = spec_b[ck, 1, at, re], spec_b[ck, 1, at, im]
            spec_a[0, at, re] = z_re * d_re + z_im * d_im
            spec_a[0, at, im] = z_re * d_im - z_im * d_re

        loop(KEPT, pointwise, 3)
        matmul(spec_a.at[0], spec_a.at[1], 1)

        def store(block, at, lanes, value):
            part_g[ck, block // ring, block % ring, at, lanes] = value

        loop(subs, lambda sub: inverse(ck, 1, sub, store))
        each(1, ring, lambda i: copy_g(ck, i).start())

    def convolutions(ck):
        drain(recv_x.at[ck, 2, pl.ds(0, ctx - 1)], sf_recv.at[ck])
        own_f(ck).wait()
        loop(subs, lambda sub: forward(ck, 2, sub))
        matmul(spec_a.at[2], spec_b.at[ck, 2], 0)

        def pointwise(k):
            at = pl.ds(k * rows, rows)
            z_re, z_im = spec_b[ck, 0, at, re], spec_b[ck, 0, at, im]
            d_re, d_im = spec_b[ck, 1, at, re], spec_b[ck, 1, at, im]
            f_re, f_im = spec_b[ck, 2, at, re], spec_b[ck, 2, at, im]
            spec_a[0, at, re] = z_re * f_re - z_im * f_im
            spec_a[0, at, im] = z_re * f_im + z_im * f_re
            spec_a[1, at, re] = f_re * d_re + f_im * d_im
            spec_a[1, at, im] = f_re * d_im - f_im * d_re

        loop(KEPT, pointwise, 3)
        loop(2, lambda sig: matmul(spec_a.at[sig], spec_a.at[sig], 1))

        def back(n):
            sig, sub = n // subs, lax.rem(n, subs)

            def store(block, at, lanes, value):
                send_y[ck, sig, block, at, lanes] = value

            inverse(ck, sig, sub, store)

        loop(2 * subs, back)
        each(1, ctx, lambda i: copy_y(ck, i).start())
        recv_y[ck, 0, me_c] = send_y[ck, 0, me_c]
        recv_y[ck, 1, me_c] = send_y[ck, 1, me_c]

        drain(recv_g.at[ck], sg_recv.at[ck])
        for part in range(PLANES):
            total = part_g[ck, part, me_z]
            for i in range(ring - 1):
                total = total + recv_g[ck, i, part]
            sum_g[ck, part] = total
        for plane, part in swaps:
            mine = is_self(plane, part)

            @pl.when(jnp.logical_not(mine))
            def _():
                copy_s(ck, plane, part).start()

            @pl.when(mine)
            def _():
                recv_s[ck, part, plane] = sum_g[ck, part]

    chunks(filter_grad)
    chunks(convolutions)

    scale = 1.0 / math.sqrt(dp * ctx * width)

    def gather(ck):
        for plane, part in swaps:

            @pl.when(jnp.logical_not(is_self(plane, part)))
            def _():
                drain(recv_s.at[ck, part, plane], ss_recv.at[ck, part, plane])

        for part in range(PLANES):
            total = recv_s[ck, part, 0]
            for plane in range(1, PLANES):
                total = total + recv_s[ck, part, plane]
            own_s[ck, part] = total * scale
        each(1, ring, lambda i: copy_a(ck, i).start())
        keep(ck).start()

    chunks(gather)

    for ck in range(CHUNKS):
        drain(recv_y.at[ck, :, pl.ds(0, ctx - 1)], sy_recv.at[ck])

    def outputs(b):
        at = pl.ds(b * share, share)
        conv = jnp.concatenate([recv_y[ck, 0, b] for ck in range(CHUNKS)], axis=0)
        dmixed = jnp.concatenate([recv_y[ck, 1, b] for ck in range(CHUNKS)], axis=0)
        out_ref[at, :] = (q_ref[at, :].astype(jnp.float32) * conv).astype(jnp.bfloat16)
        gq_ref[at, :] = (g_ref[at, :].astype(jnp.float32) * conv).astype(jnp.bfloat16)
        gk_ref[at, :] = (v_ref[at, :].astype(jnp.float32) * dmixed).astype(jnp.bfloat16)
        gv_ref[at, :] = (k_ref[at, :].astype(jnp.float32) * dmixed).astype(jnp.bfloat16)

    loop(ctx, outputs)
    saves = [
        pltpu.make_async_copy(src, dst, save_sem.at[n])
        for n, (src, dst) in enumerate(
            [(out_ref, out_hbm), (gq_ref, gq_hbm), (gk_ref, gk_hbm), (gv_ref, gv_hbm)]
        )
    ]
    for save in saves:
        save.start()

    def finish(ck):
        drain(recv_x.at[ck, pl.ds(0, 2), pl.ds(0, ctx - 1)], sx_send.at[ck])
        drain(recv_x.at[ck, 2, pl.ds(0, ctx - 1)], sf_send.at[ck])
        drain(recv_y.at[ck, :, pl.ds(0, ctx - 1)], sy_send.at[ck])
        drain(recv_g.at[ck], sg_send.at[ck])
        for plane, part in swaps:

            @pl.when(jnp.logical_not(is_self(plane, part)))
            def _():
                drain(sum_g.at[ck, part], ss_send.at[ck, plane, part])

        keep(ck).wait()
        drain(gf_ref.at[:, pl.ds(0, ring - 1), ck], sa_send.at[ck])
        drain(gf_ref.at[:, pl.ds(0, ring - 1), ck], sa_recv.at[ck])

    chunks(finish)
    for save in saves:
        save.wait()


def write_out(count, *refs):
    sources, targets, sem = refs[:count], refs[count:-1], refs[-1]
    copies = [
        pltpu.make_async_copy(sources[n], targets[n], sem.at[n]) for n in range(count)
    ]
    for copy in copies:
        copy.start()
    for copy in copies:
        copy.wait()


def shards(ctx, dp, query, key_act, value_act, filter_taps, grad_out):
    _, channels, width = query.shape
    share = channels // ctx
    rows = share // CHUNKS
    ring = dp // PLANES
    matrices, twists = tables()
    hbm = pl.BlockSpec(memory_space=pltpu.HBM)
    half = jax.ShapeDtypeStruct((channels, width), jnp.bfloat16)
    whole = jax.ShapeDtypeStruct((PLANES, ring, CHUNKS, rows, width), jnp.float32)
    dma = pltpu.SemaphoreType.DMA
    full = pltpu.VMEM((channels, width), jnp.bfloat16)
    outs = pl.pallas_call(
        functools.partial(body, ctx, dp),
        out_shape=[half] * 4 + [whole],
        in_specs=[hbm] * 7,
        out_specs=[hbm] * 5,
        scratch_shapes=[
            full,
            full,
            full,
            full,
            full,
            full,
            full,
            full,
            pltpu.VMEM(matrices.shape, jnp.bfloat16),
            pltpu.VMEM(twists.shape, jnp.float32),
            pltpu.VMEM((CHUNKS, 2, ctx, rows, width), jnp.float32),
            pltpu.VMEM((CHUNKS, 3, ctx, rows, width), jnp.float32),
            pltpu.VMEM((CHUNKS, 2, ctx, rows, width), jnp.float32),
            pltpu.VMEM((CHUNKS, 2, ctx, rows, width), jnp.float32),
            pltpu.VMEM((CHUNKS, PLANES, ring, rows, width), jnp.float32),
            pltpu.VMEM((CHUNKS, ring - 1, PLANES, rows, width), jnp.float32),
            pltpu.VMEM((CHUNKS, PLANES, rows, width), jnp.float32),
            pltpu.VMEM((CHUNKS, PLANES, PLANES, rows, width), jnp.float32),
            pltpu.VMEM((CHUNKS, PLANES, rows, width), jnp.float32),
            pltpu.VMEM((3, KEPT * rows, 2 * LANES), jnp.float32),
            pltpu.VMEM((CHUNKS, 3, KEPT * rows, 2 * LANES), jnp.float32),
            dma((6,)),
            dma((4,)),
            dma((CHUNKS,)),
            dma((CHUNKS,)),
            dma((CHUNKS,)),
            dma((CHUNKS,)),
            dma((CHUNKS,)),
            dma((CHUNKS,)),
            dma((CHUNKS,)),
            dma((CHUNKS,)),
            dma((CHUNKS,)),
            dma((CHUNKS,)),
            dma((CHUNKS, PLANES, PLANES)),
            dma((CHUNKS, PLANES, PLANES)),
            dma((CHUNKS,)),
            dma((CHUNKS,)),
        ],
        compiler_params=pltpu.CompilerParams(
            collective_id=0, has_side_effects=True, vmem_limit_bytes=GRANT
        ),
        cost_estimate=pl.CostEstimate(
            flops=3 * 2 * 6 * KEPT * share * 256 * 256, bytes_accessed=4 * 2**20, transcendentals=0
        ),
        name="hyena",
    )(
        query.reshape(channels, width),
        key_act.reshape(channels, width),
        value_act.reshape(channels, width),
        grad_out.reshape(channels, width),
        filter_taps,
        jnp.asarray(matrices),
        jnp.asarray(twists),
    )
    outs = pl.pallas_call(
        functools.partial(write_out, 5),
        out_shape=[half] * 4 + [whole],
        in_specs=[hbm] * 5,
        out_specs=[hbm] * 5,
        scratch_shapes=[dma((5,))],
        compiler_params=pltpu.CompilerParams(vmem_limit_bytes=GRANT),
        name="write_out",
    )(*outs)
    shape = query.shape
    return (
        outs[0].reshape(shape),
        outs[1].reshape(shape),
        outs[2].reshape(shape),
        outs[3].reshape(shape),
        outs[4].reshape(channels, width),
    )


def solution(mesh):
    row = P("dp", None, "ctx")
    taps = P(None, "ctx")
    return jax.shard_map(
        functools.partial(shards, mesh.shape["ctx"], mesh.shape["dp"]),
        mesh=mesh,
        in_specs=(row, row, row, taps, row),
        out_specs=(row, row, row, row, taps),
        check_vma=False,
    )
```

time: 79.7 us -> 108 us (1.36)
  the two profiles are of different devices: /device:TPU:6 before, /device:TPU:8 now
where the time goes in v2:
time: 108 us
  Pallas kernels  107 us (99%)
    pallas_call x1, Pallas kernels, shards(): pl.pallas_call(functools.partial(body, ctx, dp), out_shape=[half] * 4 + [...  58.1 us
    pallas_call x1, Pallas kernels, shards(): pl.pallas_call(functools.partial(write_out, 5), out_shape=[half] * 4 + [w...  48.8 us

profile of v2, /device:TPU:8, one launch (start us, length us, event | category | flops | bytes accessed | tf_op | source)
XLA Modules:
  0.0 107.5 jit_solution(15539744883918569787)
XLA Ops:
  0.6 58.1 %hyena.1 = (bf16[512,256]{1,0:T(8,128)(2,1)}, bf16[512,256]{1,0:T(8,128)(2,1)}, bf16[512,256]{1,0:T(8,128)(2,1)}, bf16[512,256]{1,0:T(8,128)(2,1)}, f32[2,8,2,16,256]{4,3,2,1,0:T(8,128)}) custom-call(bf16[512,256]{1,0:T(8,128)(2,1)} %bitcast.10, bf16[512,256]{1,0:T(8,128)(2,1)} %bitcast.11, bf16[512,256]{1,0:T(8,128)(2,1)} %bitcast.12, ...), custom_call_target="tpu_custom_call" | custom-call | flops 2491416576 | bytes 4194304 | tf_op jit(solution)/shard_map/hyena/pallas_call | solution.py:601
  58.7 48.8 %write_out.1 = (bf16[512,256]{1,0:T(8,128)(2,1)}, bf16[512,256]{1,0:T(8,128)(2,1)}, bf16[512,256]{1,0:T(8,128)(2,1)}, bf16[512,256]{1,0:T(8,128)(2,1)}, f32[2,8,2,16,256]{4,3,2,1,0:T(8,128)}) custom-call(bf16[512,256]{1,0:T(8,128)(2,1)} %get-tuple-element.15.refs_0_, bf16[512,256]{1,0:T(8,128)(2,1)} %get-tuple-element.16.refs_1_, ...), custom_call_target="tpu_custom_call" | custom-call | tf_op jit(solution)/shard_map/write_out/pallas_call | solution.py:661

commit v3 on v2

--- a/solution.py
+++ b/solution.py
@@ -142,7 +142,7 @@
     return matrices, twists
 
 
-CHUNKS = 2
+CHUNKS = 4
 PLANES = 2
 GRANT = 60 * 1024 * 1024
 
@@ -209,6 +209,7 @@
     subs = rows // 8
     me_p, me_z = me_d // ring, lax.rem(me_d, ring)
     c_p, c_z = me_c // ring, lax.rem(me_c, ring)
+    slot = lax.rem(me_z + ctx - me_c, ring)
 
     loads = [
         pltpu.make_async_copy(src, dst, load_sem.at[n])
@@ -240,10 +241,10 @@
         return (me_p * ring + lax.rem(me_z + i, ring), me_c)
 
     def swap_peer(plane, part):
-        return (plane * ring + c_z, part * ring + me_z)
+        return (plane * ring + me_z, part * ring + slot)
 
     def is_self(plane, part):
-        return (c_z == me_z) & (plane == me_p) & (part == c_p)
+        return (c_z == slot) & (plane == me_p) & (part == c_p)
 
     barrier = pltpu.get_barrier_semaphore()
 
@@ -274,11 +275,11 @@
 
     met = ctx - 1 + ring - 1 + len(swaps)
 
-    @pl.when(c_z == me_z)
+    @pl.when(c_z == slot)
     def _():
         pl.semaphore_wait(barrier, met - 1)
 
-    @pl.when(c_z != me_z)
+    @pl.when(c_z != slot)
     def _():
         pl.semaphore_wait(barrier, met)
 
@@ -332,7 +333,7 @@
     def copy_g(ck, i):
         peer = ring_peer(i)
         return remote(
-            part_g.at[ck, :, lax.rem(me_z + i, ring)],
+            part_g.at[ck, :, lax.rem(slot + i, ring)],
             recv_g.at[ck, i - 1],
             sg_send.at[ck],
             sg_recv.at[ck],
@@ -351,14 +352,14 @@
     def copy_a(ck, i):
         return remote(
             own_s.at[ck],
-            gf_ref.at[:, me_z, ck],
+            gf_ref.at[:, slot, ck],
             sa_send.at[ck],
             sa_recv.at[ck],
             ring_peer(i),
         )
 
     def keep(ck):
-        return pltpu.make_async_copy(own_s.at[ck], gf_ref.at[:, me_z, ck], keep_sem.at[ck])
+        return pltpu.make_async_copy(own_s.at[ck], gf_ref.at[:, slot, ck], keep_sem.at[ck])
 
     def drain(ref, sem):
         pltpu.make_async_copy(ref, ref, sem).wait()
@@ -495,9 +496,10 @@
         recv_y[ck, 0, me_c] = send_y[ck, 0, me_c]
         recv_y[ck, 1, me_c] = send_y[ck, 1, me_c]
 
+    def reduce(ck):
         drain(recv_g.at[ck], sg_recv.at[ck])
         for part in range(PLANES):
-            total = part_g[ck, part, me_z]
+            total = part_g[ck, part, slot]
             for i in range(ring - 1):
                 total = total + recv_g[ck, i, part]
             sum_g[ck, part] = total
@@ -511,9 +513,6 @@
             @pl.when(mine)
             def _():
                 recv_s[ck, part, plane] = sum_g[ck, part]
-
-    chunks(filter_grad)
-    chunks(convolutions)
 
     scale = 1.0 / math.sqrt(dp * ctx * width)
 
@@ -532,7 +531,16 @@
         each(1, ring, lambda i: copy_a(ck, i).start())
         keep(ck).start()
 
-    chunks(gather)
+    def stage(step):
+        pl.when(step < CHUNKS)(lambda: filter_grad(step))
+        pl.when((step >= 2) & (step < CHUNKS + 2))(lambda: reduce(step - 2))
+
+        @pl.when(step >= 3)
+        def _():
+            convolutions(step - 3)
+            gather(step - 3)
+
+    loop(CHUNKS + 3, stage)
 
     for ck in range(CHUNKS):
         drain(recv_y.at[ck, :, pl.ds(0, ctx - 1)], sy_recv.at[ck])
@@ -577,14 +585,21 @@
 
 
 def write_out(count, *refs):
-    sources, targets, sem = refs[:count], refs[count:-1], refs[-1]
-    copies = [
-        pltpu.make_async_copy(sources[n], targets[n], sem.at[n]) for n in range(count)
+    sources, targets = refs[:count], refs[count : 2 * count]
+    stages, sems = refs[2 * count : 3 * count], refs[3 * count]
+    reads = [
+        pltpu.make_async_copy(sources[n], stages[n], sems.at[0, n]) for n in range(count)
     ]
-    for copy in copies:
-        copy.start()
-    for copy in copies:
-        copy.wait()
+    writes = [
+        pltpu.make_async_copy(stages[n], targets[n], sems.at[1, n]) for n in range(count)
+    ]
+    for read in reads:
+        read.start()
+    for read, write in zip(reads, writes):
+        read.wait()
+        write.start()
+    for write in writes:
+        write.wait()
 
 
 def shards(ctx, dp, query, key_act, value_act, filter_taps, grad_out):
@@ -663,7 +678,7 @@
         out_shape=[half] * 4 + [whole],
         in_specs=[hbm] * 5,
         out_specs=[hbm] * 5,
-        scratch_shapes=[dma((5,))],
+        scratch_shapes=[full] * 4 + [pltpu.VMEM(whole.shape, jnp.float32), dma((2, 5))],
         compiler_params=pltpu.CompilerParams(vmem_limit_bytes=GRANT),
         name="write_out",
     )(*outs)

time: 108 us -> 49.9 us (0.46)
  the two profiles are of different devices: /device:TPU:8 before, /device:TPU:1 now
where the time goes in v3:
time: 49.9 us; the launch traced here: 49.8 us
  Pallas kernels  49.2 us (99%)
  between operations  0.64 us (1%)
    pallas_call x1, Pallas kernels, shards(): pl.pallas_call(functools.partial(body, ctx, dp), out_shape=[half] * 4 + [...  46.9 us
    pallas_call x1, Pallas kernels, shards(): pl.pallas_call(functools.partial(write_out, 5), out_shape=[half] * 4 + [w...  2.24 us

profile of v3, /device:TPU:1, one launch (start us, length us, event | category | flops | bytes accessed | tf_op | source)
XLA Modules:
  0.0 49.8 jit_solution(13623329804123311920)
XLA Ops:
  0.6 46.9 %hyena.1 = (bf16[512,256]{1,0:T(8,128)(2,1)}, bf16[512,256]{1,0:T(8,128)(2,1)}, bf16[512,256]{1,0:T(8,128)(2,1)}, bf16[512,256]{1,0:T(8,128)(2,1)}, f32[2,8,4,8,256]{4,3,2,1,0:T(8,128)}) custom-call(bf16[512,256]{1,0:T(8,128)(2,1)} %bitcast.10, bf16[512,256]{1,0:T(8,128)(2,1)} %bitcast.11, bf16[512,256]{1,0:T(8,128)(2,1)} %bitcast.12, ...), custom_call_target="tpu_custom_call" | custom-call | flops 2491416576 | bytes 4194304 | tf_op jit(solution)/shard_map/hyena/pallas_call | solution.py:616
  47.6 2.2 %write_out.1 = (bf16[512,256]{1,0:T(8,128)(2,1)}, bf16[512,256]{1,0:T(8,128)(2,1)}, bf16[512,256]{1,0:T(8,128)(2,1)}, bf16[512,256]{1,0:T(8,128)(2,1)}, f32[2,8,4,8,256]{4,3,2,1,0:T(8,128)}) custom-call(bf16[512,256]{1,0:T(8,128)(2,1)} %get-tuple-element.15.refs_0_, bf16[512,256]{1,0:T(8,128)(2,1)} %get-tuple-element.16.refs_1_, ...), custom_call_target="tpu_custom_call" | custom-call | tf_op jit(solution)/shard_map/write_out/pallas_call | solution.py:676

commit v4 on v3

--- a/solution.py
+++ b/solution.py
@@ -14,6 +14,7 @@
 RADIX = 64
 HALF = RADIX // 2
 KEPT = HALF + 1
+STRIDE = 40
 
 
 def turn(value, numerator, denominator):
@@ -139,12 +140,16 @@
     twists = np.stack(
         [np.cos(angles), np.sin(angles), np.cos(angles) * scale, np.sin(angles) * scale]
     ).astype(np.float32)
-    return matrices, twists
+    table = np.zeros((4, STRIDE, 2 * LANES), np.float32)
+    table[:, :KEPT, :LANES] = twists
+    return np.concatenate(
+        [matrices.astype(np.float32).reshape(-1, 2 * LANES), table.reshape(-1, 2 * LANES)]
+    )
 
 
 CHUNKS = 4
 PLANES = 2
-GRANT = 60 * 1024 * 1024
+GRANT = int(52.3 * 1024 * 1024)
 
 
 def body(
@@ -155,51 +160,48 @@
     v_hbm,
     g_hbm,
     f_hbm,
-    w_hbm,
-    t_hbm,
-    out_hbm,
-    gq_hbm,
-    gk_hbm,
-    gv_hbm,
-    gf_ref,
+    c_hbm,
     out_ref,
     gq_ref,
     gk_ref,
     gv_ref,
-    q_ref,
-    k_ref,
-    v_ref,
-    g_ref,
-    w_ref,
-    t_ref,
-    send_x,
-    recv_x,
-    send_y,
-    recv_y,
-    part_g,
-    recv_g,
-    sum_g,
-    recv_s,
-    own_s,
-    spec_a,
-    spec_b,
-    load_sem,
-    save_sem,
-    own_sem,
-    keep_sem,
-    sx_send,
-    sx_recv,
-    sf_send,
-    sf_recv,
-    sy_send,
-    sy_recv,
-    sg_send,
-    sg_recv,
-    ss_send,
-    ss_recv,
-    sa_send,
-    sa_recv,
+    *rest,
 ):
+    gf_refs = rest[:CHUNKS]
+    (
+        q_ref,
+        k_ref,
+        v_ref,
+        g_ref,
+        c_ref,
+        w_ref,
+        send_x,
+        recv_x,
+        send_y,
+        recv_y,
+        part_g,
+        recv_g,
+        sum_g,
+        recv_s,
+        own_s,
+        spec_a,
+        spec_b,
+        load_sem,
+        own_sem,
+        keep_sem,
+        sx_send,
+        sx_recv,
+        sf_send,
+        sf_recv,
+        sy_send,
+        sy_recv,
+        sg_send,
+        sg_recv,
+        ss_send,
+        ss_recv,
+        sa_send,
+        sa_recv,
+    ) = rest[CHUNKS:]
     me_c = lax.axis_index("ctx")
     me_d = lax.axis_index("dp")
     ring = dp // PLANES
@@ -219,8 +221,7 @@
                 (v_hbm, v_ref),
                 (q_hbm, q_ref),
                 (g_hbm, g_ref),
-                (w_hbm, w_ref),
-                (t_hbm, t_ref),
+                (c_hbm, c_ref),
             ]
         )
     ]
@@ -352,14 +353,14 @@
     def copy_a(ck, i):
         return remote(
             own_s.at[ck],
-            gf_ref.at[:, slot, ck],
+            gf_refs[ck].at[:, slot],
             sa_send.at[ck],
             sa_recv.at[ck],
             ring_peer(i),
         )
 
     def keep(ck):
-        return pltpu.make_async_copy(own_s.at[ck], gf_ref.at[:, slot, ck], keep_sem.at[ck])
+        return pltpu.make_async_copy(own_s.at[ck], gf_refs[ck].at[:, slot], keep_sem.at[ck])
 
     def drain(ref, sem):
         pltpu.make_async_copy(ref, ref, sem).wait()
@@ -377,8 +378,6 @@
         each(1, ctx, lambda i: copy_f(ck, i).start())
         own_f(ck).start()
 
-    chunks(first_f)
-
     def own_x(ck):
         recv_x[ck, 0, me_c] = send_x[ck, 0, me_c]
         recv_x[ck, 1, me_c] = send_x[ck, 1, me_c]
@@ -386,6 +385,13 @@
     chunks(own_x)
     for load in loads[4:]:
         load.wait()
+    w_ref[...] = c_ref[pl.ds(0, w_ref.shape[0]), :].astype(jnp.bfloat16)
+
+    def twist(which, k):
+        return c_ref[pl.ds(w_ref.shape[0] + which * STRIDE + k, 1), pl.ds(0, LANES)]
+
+    def weight(which):
+        return w_ref[pl.ds(which * 2 * LANES, 2 * LANES), :]
 
     re, im = pl.ds(0, LANES), pl.ds(LANES, LANES)
 
@@ -396,7 +402,7 @@
         ]
         found = padded_forward(values)
         for k in range(KEPT):
-            cos, sin = t_ref[0, pl.ds(k, 1), :], t_ref[1, pl.ds(k, 1), :]
+            cos, sin = twist(0, k), twist(1, k)
             real, imag = found[k]
             to = pl.ds(k * rows + sub * 8, 8)
             if k == 0:
@@ -412,7 +418,7 @@
     def inverse(ck, sig, sub, store):
         found = {}
         for k in range(KEPT):
-            cos, sin = t_ref[2, pl.ds(k, 1), :], t_ref[3, pl.ds(k, 1), :]
+            cos, sin = twist(2, k), twist(3, k)
             at = pl.ds(k * rows + sub * 8, 8)
             real = spec_a[sig, at, re]
             imag = spec_a[sig, at, im]
@@ -428,8 +434,8 @@
         data = src[...]
         high = data.astype(jnp.bfloat16)
         low = (data - high.astype(jnp.float32)).astype(jnp.bfloat16)
-        w_high = w_ref[2 * which]
-        w_low = w_ref[2 * which + 1]
+        w_high = weight(2 * which)
+        w_low = weight(2 * which + 1)
         dst[...] = (
             jnp.dot(high, w_high, preferred_element_type=jnp.float32)
             + jnp.dot(low, w_high, preferred_element_type=jnp.float32)
@@ -528,11 +534,16 @@
             for plane in range(1, PLANES):
                 total = total + recv_s[ck, part, plane]
             own_s[ck, part] = total * scale
-        each(1, ring, lambda i: copy_a(ck, i).start())
-        keep(ck).start()
+        for chunk in range(CHUNKS):
+
+            @pl.when(ck == chunk)
+            def _():
+                each(1, ring, lambda i: copy_a(chunk, i).start())
+                keep(chunk).start()
 
     def stage(step):
         pl.when(step < CHUNKS)(lambda: filter_grad(step))
+        pl.when(step == 1)(lambda: chunks(first_f))
         pl.when((step >= 2) & (step < CHUNKS + 2))(lambda: reduce(step - 2))
 
         @pl.when(step >= 3)
@@ -555,14 +566,6 @@
         gv_ref[at, :] = (k_ref[at, :].astype(jnp.float32) * dmixed).astype(jnp.bfloat16)
 
     loop(ctx, outputs)
-    saves = [
-        pltpu.make_async_copy(src, dst, save_sem.at[n])
-        for n, (src, dst) in enumerate(
-            [(out_ref, out_hbm), (gq_ref, gq_hbm), (gk_ref, gk_hbm), (gv_ref, gv_hbm)]
-        )
-    ]
-    for save in saves:
-        save.start()
 
     def finish(ck):
         drain(recv_x.at[ck, pl.ds(0, 2), pl.ds(0, ctx - 1)], sx_send.at[ck])
@@ -575,31 +578,28 @@
             def _():
                 drain(sum_g.at[ck, part], ss_send.at[ck, plane, part])
 
+
+    chunks(finish)
+    for ck in range(CHUNKS):
         keep(ck).wait()
-        drain(gf_ref.at[:, pl.ds(0, ring - 1), ck], sa_send.at[ck])
-        drain(gf_ref.at[:, pl.ds(0, ring - 1), ck], sa_recv.at[ck])
-
-    chunks(finish)
-    for save in saves:
-        save.wait()
+        drain(gf_refs[ck].at[:, pl.ds(0, ring - 1)], sa_send.at[ck])
+        drain(gf_refs[ck].at[:, pl.ds(0, ring - 1)], sa_recv.at[ck])
 
 
 def write_out(count, *refs):
-    sources, targets = refs[:count], refs[count : 2 * count]
-    stages, sems = refs[2 * count : 3 * count], refs[3 * count]
-    reads = [
-        pltpu.make_async_copy(sources[n], stages[n], sems.at[0, n]) for n in range(count)
+    sources, targets, sem = refs[: count + CHUNKS], refs[count + CHUNKS : -1], refs[-1]
+    copies = [
+        pltpu.make_async_copy(sources[n], targets[n], sem.at[n]) for n in range(count)
     ]
-    writes = [
-        pltpu.make_async_copy(stages[n], targets[n], sems.at[1, n]) for n in range(count)
-    ]
-    for read in reads:
-        read.start()
-    for read, write in zip(reads, writes):
-        read.wait()
-        write.start()
-    for write in writes:
-        write.wait()
+    for ck in range(CHUNKS):
+        n = count + ck
+        copies.append(
+            pltpu.make_async_copy(sources[n], targets[count].at[:, :, ck], sem.at[n])
+        )
+    for copy in copies:
+        copy.start()
+    for copy in copies:
+        copy.wait()
 
 
 def shards(ctx, dp, query, key_act, value_act, filter_taps, grad_out):
@@ -607,28 +607,26 @@
     share = channels // ctx
     rows = share // CHUNKS
     ring = dp // PLANES
-    matrices, twists = tables()
+    constants = tables()
+    vmem = pl.BlockSpec(memory_space=pltpu.VMEM)
     hbm = pl.BlockSpec(memory_space=pltpu.HBM)
     half = jax.ShapeDtypeStruct((channels, width), jnp.bfloat16)
     whole = jax.ShapeDtypeStruct((PLANES, ring, CHUNKS, rows, width), jnp.float32)
+    part = jax.ShapeDtypeStruct((PLANES, ring, rows, width), jnp.float32)
     dma = pltpu.SemaphoreType.DMA
     full = pltpu.VMEM((channels, width), jnp.bfloat16)
     outs = pl.pallas_call(
         functools.partial(body, ctx, dp),
-        out_shape=[half] * 4 + [whole],
-        in_specs=[hbm] * 7,
-        out_specs=[hbm] * 5,
+        out_shape=[half] * 4 + [part] * CHUNKS,
+        in_specs=[hbm] * 6,
+        out_specs=[vmem] * (4 + CHUNKS),
         scratch_shapes=[
             full,
             full,
             full,
             full,
-            full,
-            full,
-            full,
-            full,
-            pltpu.VMEM(matrices.shape, jnp.bfloat16),
-            pltpu.VMEM(twists.shape, jnp.float32),
+            pltpu.VMEM(constants.shape, jnp.float32),
+            pltpu.VMEM((8 * LANES, 2 * LANES), jnp.bfloat16),
             pltpu.VMEM((CHUNKS, 2, ctx, rows, width), jnp.float32),
             pltpu.VMEM((CHUNKS, 3, ctx, rows, width), jnp.float32),
             pltpu.VMEM((CHUNKS, 2, ctx, rows, width), jnp.float32),
@@ -640,8 +638,7 @@
             pltpu.VMEM((CHUNKS, PLANES, rows, width), jnp.float32),
             pltpu.VMEM((3, KEPT * rows, 2 * LANES), jnp.float32),
             pltpu.VMEM((CHUNKS, 3, KEPT * rows, 2 * LANES), jnp.float32),
-            dma((6,)),
-            dma((4,)),
+            dma((5,)),
             dma((CHUNKS,)),
             dma((CHUNKS,)),
             dma((CHUNKS,)),
@@ -670,16 +667,15 @@
         value_act.reshape(channels, width),
         grad_out.reshape(channels, width),
         filter_taps,
-        jnp.asarray(matrices),
-        jnp.asarray(twists),
+        jnp.asarray(constants),
     )
     outs = pl.pallas_call(
-        functools.partial(write_out, 5),
+        functools.partial(write_out, 4),
         out_shape=[half] * 4 + [whole],
-        in_specs=[hbm] * 5,
+        in_specs=[vmem] * (4 + CHUNKS),
         out_specs=[hbm] * 5,
-        scratch_shapes=[full] * 4 + [pltpu.VMEM(whole.shape, jnp.float32), dma((2, 5))],
-        compiler_params=pltpu.CompilerParams(vmem_limit_bytes=GRANT),
+        scratch_shapes=[dma((4 + CHUNKS,))],
+        compiler_params=pltpu.CompilerParams(vmem_limit_bytes=4 * 1024 * 1024),
         name="write_out",
     )(*outs)
     shape = query.shape

time: 49.9 us -> 48.1 us (0.964)
  the two profiles are of different devices: /device:TPU:1 before, /device:TPU:6 now
where the time goes in v4:
time: 48.1 us; the launch traced here: 47.2 us
  Pallas kernels  46.6 us (97%)
  between operations  0.64 us (1%)
    pallas_call x1, Pallas kernels, shards(): pl.pallas_call(functools.partial(body, ctx, dp), out_shape=[half] * 4 + [...  45.4 us
    pallas_call x1, Pallas kernels, shards(): pl.pallas_call(functools.partial(write_out, 4), out_shape=[half] * 4 + [w...  1.2 us

profile of v4, /device:TPU:6, one launch (start us, length us, event | category | flops | bytes accessed | tf_op | source)
XLA Modules:
  0.0 47.2 jit_solution(6605056144151040608)
XLA Ops:
  0.6 45.4 %hyena.1 = (bf16[512,256]{1,0:T(8,128)(2,1)S(1)}, bf16[512,256]{1,0:T(8,128)(2,1)S(1)}, bf16[512,256]{1,0:T(8,128)(2,1)S(1)}, bf16[512,256]{1,0:T(8,128)(2,1)S(1...) custom-call(bf16[512,256]{1,0:T(8,128)(2,1)} %bitcast.10, ...), custom_call_target="tpu_custom_call" | custom-call | flops 2491416576 | bytes 4194304 | tf_op jit(solution)/shard_map/hyena/pallas_call | solution.py:618
  46.0 1.2 %write_out.1 = (bf16[512,256]{1,0:T(8,128)(2,1)}, bf16[512,256]{1,0:T(8,128)(2,1)}, bf16[512,256]{1,0:T(8,128)(2,1)}, bf16[512,256]{1,0:T(8,128)(2,1)}, f32[2,8,4,8,256]{4,3,2,1,0:T(8,128)}) custom-call(bf16[512,256]{1,0:T(8,128)(2,1)S(1)} %get-tuple-element.18.refs_0_, bf16[512,256]{1,0:T(8,128)(2,1)S(1)} %get-tuple-element.19.refs_1_, ...), custom_call_target="tpu_custom_call" | custom-call | tf_op jit(solution)/shard_map/write_out/pallas_call | solution.py:672

commit v5 on v4

--- a/solution.py
+++ b/solution.py
@@ -186,6 +186,8 @@
         own_s,
         spec_a,
         spec_b,
+        plane_sem,
+        go_sem,
         load_sem,
         own_sem,
         keep_sem,
@@ -249,16 +251,17 @@
 
     barrier = pltpu.get_barrier_semaphore()
 
-    def greet(peer):
-        pl.semaphore_signal(barrier, inc=1, device_id=peer, device_id_type=MESH)
-
-    each(1, ctx, lambda i: greet(ctx_peer(i)))
-    each(1, ring, lambda i: greet(ring_peer(i)))
+    def signal(sem, peer):
+        pl.semaphore_signal(sem, inc=1, device_id=peer, device_id_type=MESH)
+
+    leads = me_c == 0
+
+    def greet(i):
+        peer = ctx_peer(i)
+        pl.when(peer[1] != 0)(lambda: signal(barrier, peer))
+
+    each(1, ctx, greet)
     swaps = [(plane, part) for plane in range(PLANES) for part in range(PLANES)]
-    for plane, part in swaps:
-        pl.when(jnp.logical_not(is_self(plane, part)))(
-            functools.partial(greet, swap_peer(plane, part))
-        )
 
     for load in loads[:4]:
         load.wait()
@@ -274,15 +277,18 @@
 
     lax.fori_loop(0, ctx, products, 0)
 
-    met = ctx - 1 + ring - 1 + len(swaps)
-
-    @pl.when(c_z == slot)
+    @pl.when(jnp.logical_not(leads))
     def _():
-        pl.semaphore_wait(barrier, met - 1)
-
-    @pl.when(c_z != slot)
+        pl.semaphore_wait(barrier, ctx - 1)
+
+    pl.when(me_c == 1)(lambda: signal(plane_sem, (me_d, 0)))
+
+    @pl.when(leads)
     def _():
-        pl.semaphore_wait(barrier, met)
+        pl.semaphore_wait(plane_sem, 1)
+        each(1, ring, lambda i: signal(barrier, ring_peer(i)))
+        for plane in range(PLANES):
+            pl.when(plane != me_p)(lambda: signal(barrier, (plane * ring + me_z, me_c)))
 
     def remote(src, dst, send, recv, peer):
         return pltpu.make_async_remote_copy(
@@ -373,6 +379,12 @@
         lax.fori_loop(0, CHUNKS, step, 0)
 
     chunks(lambda ck: each(1, ctx, lambda i: copy_x(ck, i).start()))
+
+    @pl.when(leads)
+    def _():
+        pl.semaphore_wait(barrier, ring - 1 + PLANES - 1)
+        each(1, ctx, lambda i: signal(go_sem, ctx_peer(i)))
+
 
     def first_f(ck):
         each(1, ctx, lambda i: copy_f(ck, i).start())
@@ -431,16 +443,17 @@
             store(n // 2, pl.ds(sub * 8, 8), pl.ds((n % 2) * LANES, LANES), values[n])
 
     def matmul(src, dst, which):
-        data = src[...]
+        data = src[...].reshape(-1, 2 * LANES)
+        height = data.shape[0]
         high = data.astype(jnp.bfloat16)
         low = (data - high.astype(jnp.float32)).astype(jnp.bfloat16)
-        w_high = weight(2 * which)
-        w_low = weight(2 * which + 1)
-        dst[...] = (
-            jnp.dot(high, w_high, preferred_element_type=jnp.float32)
-            + jnp.dot(low, w_high, preferred_element_type=jnp.float32)
-            + jnp.dot(high, w_low, preferred_element_type=jnp.float32)
-        )
+        both = jnp.dot(
+            jnp.concatenate([high, low], axis=0),
+            weight(2 * which),
+            preferred_element_type=jnp.float32,
+        )
+        rest = jnp.dot(high, weight(2 * which + 1), preferred_element_type=jnp.float32)
+        dst[...] = (both[:height] + both[height:] + rest).reshape(dst.shape)
 
     def loop(count, act, unroll=1):
         def step(i, carry):
@@ -452,7 +465,7 @@
     def filter_grad(ck):
         drain(recv_x.at[ck, pl.ds(0, 2), pl.ds(0, ctx - 1)], sx_recv.at[ck])
         loop(2 * subs, lambda n: forward(ck, n // subs, lax.rem(n, subs)))
-        loop(2, lambda sig: matmul(spec_a.at[sig], spec_b.at[ck, sig], 0))
+        matmul(spec_a.at[pl.ds(0, 2)], spec_b.at[ck, pl.ds(0, 2)], 0)
 
         def pointwise(k):
             at = pl.ds(k * rows, rows)
@@ -461,13 +474,18 @@
             spec_a[0, at, re] = z_re * d_re + z_im * d_im
             spec_a[0, at, im] = z_re * d_im - z_im * d_re
 
-        loop(KEPT, pointwise, 3)
+        loop(KEPT, pointwise, 11)
         matmul(spec_a.at[0], spec_a.at[1], 1)
 
         def store(block, at, lanes, value):
             part_g[ck, block // ring, block % ring, at, lanes] = value
 
         loop(subs, lambda sub: inverse(ck, 1, sub, store))
+
+        @pl.when((ck == 0) & jnp.logical_not(leads))
+        def _():
+            pl.semaphore_wait(go_sem, 1)
+
         each(1, ring, lambda i: copy_g(ck, i).start())
 
     def convolutions(ck):
@@ -486,8 +504,8 @@
             spec_a[1, at, re] = f_re * d_re + f_im * d_im
             spec_a[1, at, im] = f_re * d_im - f_im * d_re
 
-        loop(KEPT, pointwise, 3)
-        loop(2, lambda sig: matmul(spec_a.at[sig], spec_a.at[sig], 1))
+        loop(KEPT, pointwise, 11)
+        matmul(spec_a.at[pl.ds(0, 2)], spec_a.at[pl.ds(0, 2)], 1)
 
         def back(n):
             sig, sub = n // subs, lax.rem(n, subs)
@@ -638,6 +656,8 @@
             pltpu.VMEM((CHUNKS, PLANES, rows, width), jnp.float32),
             pltpu.VMEM((3, KEPT * rows, 2 * LANES), jnp.float32),
             pltpu.VMEM((CHUNKS, 3, KEPT * rows, 2 * LANES), jnp.float32),
+            pltpu.SemaphoreType.REGULAR,
+            pltpu.SemaphoreType.REGULAR,
             dma((5,)),
             dma((CHUNKS,)),
             dma((CHUNKS,)),

time: 48.1 us -> 46.7 us (0.971); the launches traced: 47.2 us -> 46.6 us
  Pallas kernels: 46.6 us -> 45.9 us
    pallas_call x1, Pallas kernels: 45.4 us -> 44.7 us  [shards(): pl.pallas_call(functools.partial(body, ctx, dp), out_shape=[half] * 4 + [...]
where the time goes in v5:
time: 46.7 us; the launch traced here: 46.6 us
  Pallas kernels  45.9 us (98%)
  between operations  0.64 us (1%)
    pallas_call x1, Pallas kernels, shards(): pl.pallas_call(functools.partial(body, ctx, dp), out_shape=[half] * 4 + [...  44.7 us
    pallas_call x1, Pallas kernels, shards(): pl.pallas_call(functools.partial(write_out, 4), out_shape=[half] * 4 + [w...  1.2 us

profile of v5, /device:TPU:6, one launch (start us, length us, event | category | flops | bytes accessed | tf_op | source)
XLA Modules:
  0.0 46.6 jit_solution(16750913647105633471)
XLA Ops:
  0.6 44.7 %hyena.1 = (bf16[512,256]{1,0:T(8,128)(2,1)S(1)}, bf16[512,256]{1,0:T(8,128)(2,1)S(1)}, bf16[512,256]{1,0:T(8,128)(2,1)S(1)}, bf16[512,256]{1,0:T(8,128)(2,1)S(1...) custom-call(bf16[512,256]{1,0:T(8,128)(2,1)} %bitcast.10, ...), custom_call_target="tpu_custom_call" | custom-call | flops 2491416576 | bytes 4194304 | tf_op jit(solution)/shard_map/hyena/pallas_call | solution.py:636
  45.4 1.2 %write_out.1 = (bf16[512,256]{1,0:T(8,128)(2,1)}, bf16[512,256]{1,0:T(8,128)(2,1)}, bf16[512,256]{1,0:T(8,128)(2,1)}, bf16[512,256]{1,0:T(8,128)(2,1)}, f32[2,8,4,8,256]{4,3,2,1,0:T(8,128)}) custom-call(bf16[512,256]{1,0:T(8,128)(2,1)S(1)} %get-tuple-element.18.refs_0_, bf16[512,256]{1,0:T(8,128)(2,1)S(1)} %get-tuple-element.19.refs_1_, ...), custom_call_target="tpu_custom_call" | custom-call | tf_op jit(solution)/shard_map/write_out/pallas_call | solution.py:692

commit v6 on v5

--- a/solution.py
+++ b/solution.py
@@ -560,8 +560,8 @@
                 keep(chunk).start()
 
     def stage(step):
+        pl.when(step < CHUNKS)(lambda: first_f(step))
         pl.when(step < CHUNKS)(lambda: filter_grad(step))
-        pl.when(step == 1)(lambda: chunks(first_f))
         pl.when((step >= 2) & (step < CHUNKS + 2))(lambda: reduce(step - 2))
 
         @pl.when(step >= 3)

time: 46.7 us -> 45.4 us (0.972)
  Pallas kernels: 45.9 us -> 44.5 us
    pallas_call x1, Pallas kernels: 44.7 us -> 43.3 us  [shards(): pl.pallas_call(functools.partial(body, ctx, dp), out_shape=[half] * 4 + [...]
where the time goes in v6:
time: 45.4 us; the launch traced here: 45.2 us
  Pallas kernels  44.5 us (98%)
  between operations  0.64 us (1%)
    pallas_call x1, Pallas kernels, shards(): pl.pallas_call(functools.partial(body, ctx, dp), out_shape=[half] * 4 + [...  43.3 us
    pallas_call x1, Pallas kernels, shards(): pl.pallas_call(functools.partial(write_out, 4), out_shape=[half] * 4 + [w...  1.2 us

profile of v6, /device:TPU:6, one launch (start us, length us, event | category | flops | bytes accessed | tf_op | source)
XLA Modules:
  0.0 45.2 jit_solution(10947570367891659739)
XLA Ops:
  0.6 43.3 %hyena.1 = (bf16[512,256]{1,0:T(8,128)(2,1)S(1)}, bf16[512,256]{1,0:T(8,128)(2,1)S(1)}, bf16[512,256]{1,0:T(8,128)(2,1)S(1)}, bf16[512,256]{1,0:T(8,128)(2,1)S(1...) custom-call(bf16[512,256]{1,0:T(8,128)(2,1)} %bitcast.10, ...), custom_call_target="tpu_custom_call" | custom-call | flops 2491416576 | bytes 4194304 | tf_op jit(solution)/shard_map/hyena/pallas_call | solution.py:636
  44.0 1.2 %write_out.1 = (bf16[512,256]{1,0:T(8,128)(2,1)}, bf16[512,256]{1,0:T(8,128)(2,1)}, bf16[512,256]{1,0:T(8,128)(2,1)}, bf16[512,256]{1,0:T(8,128)(2,1)}, f32[2,8,4,8,256]{4,3,2,1,0:T(8,128)}) custom-call(bf16[512,256]{1,0:T(8,128)(2,1)S(1)} %get-tuple-element.18.refs_0_, bf16[512,256]{1,0:T(8,128)(2,1)S(1)} %get-tuple-element.19.refs_1_, ...), custom_call_target="tpu_custom_call" | custom-call | tf_op jit(solution)/shard_map/write_out/pallas_call | solution.py:692

commit v7 on v6

--- a/solution.py
+++ b/solution.py
@@ -230,12 +230,18 @@
     for load in loads:
         load.start()
 
+    far_first = sorted(range(1, ring), key=lambda i: -min(i, ring - i))
+
     def each(first, last, act):
         def step(i, carry):
             act(i)
             return carry
 
         lax.fori_loop(first, last, step, 0, unroll=True)
+
+    def outward(act):
+        for i in sorted(range(1, ctx), key=lambda i: -min(i, ctx - i)):
+            act(i)
 
     def ctx_peer(i):
         return (me_d, lax.rem(me_c + i, ctx))
@@ -327,11 +333,11 @@
             own_sem.at[ck],
         )
 
-    def copy_y(ck, i):
+    def copy_y(ck, sig, i):
         peer = ctx_peer(i)
         return remote(
-            send_y.at[ck, :, peer[1]],
-            recv_y.at[ck, :, me_c],
+            send_y.at[ck, sig, peer[1]],
+            recv_y.at[ck, sig, me_c],
             sy_send.at[ck],
             sy_recv.at[ck],
             peer,
@@ -378,7 +384,7 @@
 
         lax.fori_loop(0, CHUNKS, step, 0)
 
-    chunks(lambda ck: each(1, ctx, lambda i: copy_x(ck, i).start()))
+    chunks(lambda ck: outward(lambda i: copy_x(ck, i).start()))
 
     @pl.when(leads)
     def _():
@@ -387,7 +393,7 @@
 
 
     def first_f(ck):
-        each(1, ctx, lambda i: copy_f(ck, i).start())
+        outward(lambda i: copy_f(ck, i).start())
         own_f(ck).start()
 
     def own_x(ck):
@@ -486,7 +492,8 @@
         def _():
             pl.semaphore_wait(go_sem, 1)
 
-        each(1, ring, lambda i: copy_g(ck, i).start())
+        for i in far_first:
+            copy_g(ck, i).start()
 
     def convolutions(ck):
         drain(recv_x.at[ck, 2, pl.ds(0, ctx - 1)], sf_recv.at[ck])
@@ -515,8 +522,9 @@
 
             inverse(ck, sig, sub, store)
 
-        loop(2 * subs, back)
-        each(1, ctx, lambda i: copy_y(ck, i).start())
+        for sig in range(2):
+            loop(subs, lambda sub: back(sig * subs + sub))
+            outward(lambda i: copy_y(ck, sig, i).start())
         recv_y[ck, 0, me_c] = send_y[ck, 0, me_c]
         recv_y[ck, 1, me_c] = send_y[ck, 1, me_c]
 
@@ -527,7 +535,8 @@
             for i in range(ring - 1):
                 total = total + recv_g[ck, i, part]
             sum_g[ck, part] = total
-        for plane, part in swaps:
+        for step, part in swaps:
+            plane = lax.rem(me_p + 1 + step, PLANES)
             mine = is_self(plane, part)
 
             @pl.when(jnp.logical_not(mine))
@@ -556,7 +565,8 @@
 
             @pl.when(ck == chunk)
             def _():
-                each(1, ring, lambda i: copy_a(chunk, i).start())
+                for i in far_first:
+                    copy_a(chunk, i).start()
                 keep(chunk).start()
 
     def stage(step):

time: 45.4 us -> 44.3 us (0.976); the launches traced: 45.2 us -> 43.5 us
  Pallas kernels: 44.5 us -> 42.9 us
    pallas_call x1, Pallas kernels: 43.3 us -> 41.7 us  [shards(): pl.pallas_call(functools.partial(body, ctx, dp), out_shape=[half] * 4 + [...]
where the time goes in v7:
time: 44.3 us; the launch traced here: 43.5 us
  Pallas kernels  42.9 us (97%)
  between operations  0.64 us (1%)
    pallas_call x1, Pallas kernels, shards(): pl.pallas_call(functools.partial(body, ctx, dp), out_shape=[half] * 4 + [...  41.7 us
    pallas_call x1, Pallas kernels, shards(): pl.pallas_call(functools.partial(write_out, 4), out_shape=[half] * 4 + [w...  1.2 us

profile of v7, /device:TPU:6, one launch (start us, length us, event | category | flops | bytes accessed | tf_op | source)
XLA Modules:
  0.0 43.5 jit_solution(16915424487872543296)
XLA Ops:
  0.6 41.7 %hyena.1 = (bf16[512,256]{1,0:T(8,128)(2,1)S(1)}, bf16[512,256]{1,0:T(8,128)(2,1)S(1)}, bf16[512,256]{1,0:T(8,128)(2,1)S(1)}, bf16[512,256]{1,0:T(8,128)(2,1)S(1...) custom-call(bf16[512,256]{1,0:T(8,128)(2,1)} %bitcast.10, ...), custom_call_target="tpu_custom_call" | custom-call | flops 2491416576 | bytes 4194304 | tf_op jit(solution)/shard_map/hyena/pallas_call | solution.py:646
  42.3 1.2 %write_out.1 = (bf16[512,256]{1,0:T(8,128)(2,1)}, bf16[512,256]{1,0:T(8,128)(2,1)}, bf16[512,256]{1,0:T(8,128)(2,1)}, bf16[512,256]{1,0:T(8,128)(2,1)}, f32[2,8,4,8,256]{4,3,2,1,0:T(8,128)}) custom-call(bf16[512,256]{1,0:T(8,128)(2,1)S(1)} %get-tuple-element.18.refs_0_, bf16[512,256]{1,0:T(8,128)(2,1)S(1)} %get-tuple-element.19.refs_1_, ...), custom_call_target="tpu_custom_call" | custom-call | tf_op jit(solution)/shard_map/write_out/pallas_call | solution.py:702

commit v8 on v7

--- a/solution.py
+++ b/solution.py
@@ -339,7 +339,7 @@
             send_y.at[ck, sig, peer[1]],
             recv_y.at[ck, sig, me_c],
             sy_send.at[ck],
-            sy_recv.at[ck],
+            sy_recv.at[ck, sig],
             peer,
         )
 
@@ -581,19 +581,22 @@
 
     loop(CHUNKS + 3, stage)
 
-    for ck in range(CHUNKS):
-        drain(recv_y.at[ck, :, pl.ds(0, ctx - 1)], sy_recv.at[ck])
-
-    def outputs(b):
-        at = pl.ds(b * share, share)
-        conv = jnp.concatenate([recv_y[ck, 0, b] for ck in range(CHUNKS)], axis=0)
-        dmixed = jnp.concatenate([recv_y[ck, 1, b] for ck in range(CHUNKS)], axis=0)
-        out_ref[at, :] = (q_ref[at, :].astype(jnp.float32) * conv).astype(jnp.bfloat16)
-        gq_ref[at, :] = (g_ref[at, :].astype(jnp.float32) * conv).astype(jnp.bfloat16)
-        gk_ref[at, :] = (v_ref[at, :].astype(jnp.float32) * dmixed).astype(jnp.bfloat16)
-        gv_ref[at, :] = (k_ref[at, :].astype(jnp.float32) * dmixed).astype(jnp.bfloat16)
-
-    loop(ctx, outputs)
+    def outputs(pair, sig):
+        for ck in (pair, pair + 1):
+            drain(recv_y.at[ck, sig, pl.ds(0, ctx - 1)], sy_recv.at[ck, sig])
+        gates = [(q_ref, out_ref), (g_ref, gq_ref)] if sig == 0 else [(v_ref, gk_ref), (k_ref, gv_ref)]
+
+        def block(b):
+            at = pl.ds(b * share + pair * rows, 2 * rows)
+            value = jnp.concatenate([recv_y[pair, sig, b], recv_y[pair + 1, sig, b]], axis=0)
+            for gate, to in gates:
+                to[at, :] = (gate[at, :].astype(jnp.float32) * value).astype(jnp.bfloat16)
+
+        loop(ctx, block, 4)
+
+    for pair in range(0, CHUNKS, 2):
+        for sig in range(2):
+            outputs(pair, sig)
 
     def finish(ck):
         drain(recv_x.at[ck, pl.ds(0, 2), pl.ds(0, ctx - 1)], sx_send.at[ck])
@@ -676,7 +679,7 @@
             dma((CHUNKS,)),
             dma((CHUNKS,)),
             dma((CHUNKS,)),
-            dma((CHUNKS,)),
+            dma((CHUNKS, 2)),
             dma((CHUNKS,)),
             dma((CHUNKS,)),
             dma((CHUNKS, PLANES, PLANES)),

time: 44.3 us -> 44.3 us (level)
  no operation moved by 1% of the time
where the time goes in v8:
time: 44.3 us; the launch traced here: 43.6 us
  Pallas kernels  42.9 us (97%)
  between operations  0.64 us (1%)
    pallas_call x1, Pallas kernels, shards(): pl.pallas_call(functools.partial(body, ctx, dp), out_shape=[half] * 4 + [...  41.7 us
    pallas_call x1, Pallas kernels, shards(): pl.pallas_call(functools.partial(write_out, 4), out_shape=[half] * 4 + [w...  1.2 us

profile of v8, /device:TPU:6, one launch (start us, length us, event | category | flops | bytes accessed | tf_op | source)
XLA Modules:
  0.0 43.6 jit_solution(1969733914512492324)
XLA Ops:
  0.6 41.7 %hyena.1 = (bf16[512,256]{1,0:T(8,128)(2,1)S(1)}, bf16[512,256]{1,0:T(8,128)(2,1)S(1)}, bf16[512,256]{1,0:T(8,128)(2,1)S(1)}, bf16[512,256]{1,0:T(8,128)(2,1)S(1...) custom-call(bf16[512,256]{1,0:T(8,128)(2,1)} %bitcast.10, ...), custom_call_target="tpu_custom_call" | custom-call | flops 2491416576 | bytes 4194304 | tf_op jit(solution)/shard_map/hyena/pallas_call | solution.py:649
  42.4 1.2 %write_out.1 = (bf16[512,256]{1,0:T(8,128)(2,1)}, bf16[512,256]{1,0:T(8,128)(2,1)}, bf16[512,256]{1,0:T(8,128)(2,1)}, bf16[512,256]{1,0:T(8,128)(2,1)}, f32[2,8,4,8,256]{4,3,2,1,0:T(8,128)}) custom-call(bf16[512,256]{1,0:T(8,128)(2,1)S(1)} %get-tuple-element.18.refs_0_, bf16[512,256]{1,0:T(8,128)(2,1)S(1)} %get-tuple-element.19.refs_1_, ...), custom_call_target="tpu_custom_call" | custom-call | tf_op jit(solution)/shard_map/write_out/pallas_call | solution.py:705

commit v9 on v8

--- a/solution.py
+++ b/solution.py
@@ -535,17 +535,17 @@
             for i in range(ring - 1):
                 total = total + recv_g[ck, i, part]
             sum_g[ck, part] = total
-        for step, part in swaps:
-            plane = lax.rem(me_p + 1 + step, PLANES)
-            mine = is_self(plane, part)
-
-            @pl.when(jnp.logical_not(mine))
-            def _():
-                copy_s(ck, plane, part).start()
-
-            @pl.when(mine)
-            def _():
-                recv_s[ck, part, plane] = sum_g[ck, part]
+            for step in range(PLANES):
+                plane = lax.rem(me_p + 1 + step, PLANES)
+                mine = is_self(plane, part)
+
+                @pl.when(jnp.logical_not(mine))
+                def _():
+                    copy_s(ck, plane, part).start()
+
+                @pl.when(mine)
+                def _():
+                    recv_s[ck, part, plane] = sum_g[ck, part]
 
     scale = 1.0 / math.sqrt(dp * ctx * width)
 

time: 44.3 us -> 44.3 us (level)
  no operation moved by 1% of the time
where the time goes in v9:
time: 44.3 us; the launch traced here: 43.6 us
  Pallas kernels  42.9 us (97%)
  between operations  0.64 us (1%)
    pallas_call x1, Pallas kernels, shards(): pl.pallas_call(functools.partial(body, ctx, dp), out_shape=[half] * 4 + [...  41.7 us
    pallas_call x1, Pallas kernels, shards(): pl.pallas_call(functools.partial(write_out, 4), out_shape=[half] * 4 + [w...  1.2 us

profile of v9, /device:TPU:6, one launch (start us, length us, event | category | flops | bytes accessed | tf_op | source)
XLA Modules:
  0.0 43.6 jit_solution(13647408467396033016)
XLA Ops:
  0.6 41.7 %hyena.1 = (bf16[512,256]{1,0:T(8,128)(2,1)S(1)}, bf16[512,256]{1,0:T(8,128)(2,1)S(1)}, bf16[512,256]{1,0:T(8,128)(2,1)S(1)}, bf16[512,256]{1,0:T(8,128)(2,1)S(1...) custom-call(bf16[512,256]{1,0:T(8,128)(2,1)} %bitcast.10, ...), custom_call_target="tpu_custom_call" | custom-call | flops 2491416576 | bytes 4194304 | tf_op jit(solution)/shard_map/hyena/pallas_call | solution.py:649
  42.4 1.2 %write_out.1 = (bf16[512,256]{1,0:T(8,128)(2,1)}, bf16[512,256]{1,0:T(8,128)(2,1)}, bf16[512,256]{1,0:T(8,128)(2,1)}, bf16[512,256]{1,0:T(8,128)(2,1)}, f32[2,8,4,8,256]{4,3,2,1,0:T(8,128)}) custom-call(bf16[512,256]{1,0:T(8,128)(2,1)S(1)} %get-tuple-element.18.refs_0_, bf16[512,256]{1,0:T(8,128)(2,1)S(1)} %get-tuple-element.19.refs_1_, ...), custom_call_target="tpu_custom_call" | custom-call | tf_op jit(solution)/shard_map/write_out/pallas_call | solution.py:705
